TPU v7x, 128 devices: a whole 4x4x4 slice. The times are simulated.
128 devices in a mesh: occi: 8 (over y, core), occj: 16 (over z, x).
Axes of the slice: x: 4, y: 4, z: 4, core: 2. Of those that a mesh axis runs over, the one named last changes fastest.
Arguments:
- factors: float32 [128, 512, 256], P(('occi', 'occj')), may hold values from -6 to 6
- pno_vecs: float32 [8192, 256, 128], P(('occi', 'occj')), may hold values from -0.09375 to 0.09375
- pair_occ: int32 [8192, 2], P(('occi', 'occj')), may hold values from 0 to 127, as said below
- pno_count: int32 [8192], P(('occi', 'occj')), may hold values from 32 to 128, as said below
- pno_energy: float32 [8192, 128], P(('occi', 'occj')), may hold values from 0.3 to 3
- occ_energy: float32 [128], replicated, may hold values from -1.5 to -0.3
- coupi_peer: int32 [4096, 1], P(('occi', 'occj')), may hold values from 0 to 7; in each aligned block of 32 rows (0 to 31, 32 to 63, ...) at most 8 rows name the same one
- coupi_slot: int32 [4096], P(('occi', 'occj')), may hold values from 0 to 63
- coupi_target: int32 [4096], P(('occi', 'occj')), may hold values from 0 to 63
- coupi_fock: float32 [4096], P(('occi', 'occj')), may hold values from -0.5 to 0.5
- coupi_correlation: float32 [4096, 128, 128], P(('occi', 'occj')), may hold values from -0.15 to 1, as said below
- coupj_peer: int32 [4096, 1], P(('occi', 'occj')), may hold values from 0 to 15; in each aligned block of 32 rows (0 to 31, 32 to 63, ...) at most 4 rows name the same one
- coupj_slot: int32 [4096], P(('occi', 'occj')), may hold values from 0 to 63
- coupj_target: int32 [4096], P(('occi', 'occj')), may hold values from 0 to 63
- coupj_fock: float32 [4096], P(('occi', 'occj')), may hold values from -0.5 to 0.5
- coupj_correlation: float32 [4096, 128, 128], P(('occi', 'occj')), may hold values from -0.15 to 1, as said below
Outputs:
- amplitude: float32 [8192, 128, 128], P(('occi', 'occj'))
- residual: float32 [8192, 128, 128], P(('occi', 'occj'))
Inputs may be any that keep to these rules, and one draw needn't show every extreme that they name: `pair_occ`: the pairs in the rows of one device have their first orbital in that device's occi block of 1 * 16 orbitals starting at u * 16, and their second orbital o in its occj block: (o) % 16 equals the device's occj index. `pno_count`: pair 0 uses all 128 natural orbitals. `coupi_peer`: in the rows of one device no peer index appears more than 8 times. `coupj_peer`: in the rows of one device no peer index appears more than 4 times. `coupi_correlation`: diagonal entries lie in 0.5 to 1. `coupj_correlation`: diagonal entries lie in 0.5 to 1.
All inputs are finite; a program needn't handle non-finite values.
Results may differ from a plain program's by a relative error of at most 0.0003.
Values sent between devices are 32-bit elements; how exact they have to be, the bound alone decides.
A program may use at most 128 MiB of HBM per device.

v0:
```python
import jax
import jax.numpy as jnp
from jax import lax
from jax.sharding import PartitionSpec as P

ITERS = 2


def arrange(peer_column, source_slot, peer_count):
    coupling_count = peer_column.shape[0]
    capacity = max(2, 2 * coupling_count // peer_count)
    member = (peer_column[:, None] == jnp.arange(peer_count)[None, :]).astype(jnp.int32)
    before = jnp.cumsum(member, axis=0) - member
    position = peer_column * capacity + jnp.sum(before * member, axis=1)
    matches = position[:, None] == jnp.arange(peer_count * capacity)[None, :]
    requests = jnp.sum(jnp.where(matches, source_slot[:, None] + 1, 0), axis=0) - 1
    return (position, requests.reshape(peer_count, capacity))


def select_rows(amplitude, incoming):
    source_rows = jnp.maximum(incoming.reshape(-1), 0)
    return amplitude[source_rows].reshape(incoming.shape + amplitude.shape[1:])


def apply_terms(correlation, source, fock):
    highest = lax.Precision.HIGHEST
    half_done = jnp.einsum("cab,cbd->cad", correlation, source, precision=highest)
    transformed = jnp.einsum("cad,ced->cae", half_done, correlation, precision=highest)
    return transformed * fock[:, None, None]


def scatter_terms(target_rows, coupling_terms):
    return jnp.einsum("cp,cab->pab", target_rows, coupling_terms, precision=lax.Precision.HIGHEST)


def local(
    factors,
    pno_vecs,
    pair_occ,
    pno_count,
    pno_energy,
    occ_energy,
    coupi_peer,
    coupi_slot,
    coupi_target,
    coupi_fock,
    coupi_correlation,
    coupj_peer,
    coupj_slot,
    coupj_target,
    coupj_fock,
    coupj_correlation,
):
    highest = lax.Precision.HIGHEST
    first_size = lax.axis_size("occi")
    second_size = lax.axis_size("occj")
    first_index = lax.axis_index("occi")
    owned = factors.shape[0]
    block_first = lax.all_gather(factors, "occj", axis=0, tiled=True)
    block_second = lax.all_gather(factors, "occi", axis=0, tiled=True)
    local_first = pair_occ[:, 0] - first_index * owned * second_size
    global_second = pair_occ[:, 1]
    local_second = global_second // owned // second_size * owned + global_second % owned
    pair_count, vir_width, pno_width = pno_vecs.shape

    def integrals(inputs):
        rows_first, rows_second, vectors = inputs
        left_factor = block_first[rows_first]
        right_factor = block_second[rows_second]
        left_half = jnp.einsum("gqv,gva->gqa", left_factor, vectors, precision=highest)
        right_half = jnp.einsum("gqv,gva->gqa", right_factor, vectors, precision=highest)
        return jnp.einsum("gqa,gqb->gab", left_half, right_half, precision=highest)

    position_i, requests_i = arrange(coupi_peer[:, 0], coupi_slot, first_size)
    position_j, requests_j = arrange(coupj_peer[:, 0], coupj_slot, second_size)
    incoming_i = lax.all_to_all(requests_i, "occi", split_axis=0, concat_axis=0, tiled=True)
    incoming_j = lax.all_to_all(requests_j, "occj", split_axis=0, concat_axis=0, tiled=True)
    target_rows_i = (coupi_target[:, None] == jnp.arange(pair_count)[None, :]).astype(jnp.float32)
    target_rows_j = (coupj_target[:, None] == jnp.arange(pair_count)[None, :]).astype(jnp.float32)
    rows = jnp.arange(pair_count)
    row_count = rows.shape[0]
    padded_count = (row_count + 7) // 8 * 8
    padded_rows = jnp.concatenate([rows, jnp.zeros((padded_count - row_count,), jnp.int32)])
    group_count = padded_count // 8
    integral = lax.map(
        integrals,
        (
            local_first[padded_rows].reshape(group_count, 8),
            local_second[padded_rows].reshape(group_count, 8),
            pno_vecs[padded_rows].reshape(group_count, 8, vir_width, pno_width),
        ),
    )
    integral = integral.reshape(padded_count, pno_width, pno_width)
    live_pno = (jnp.arange(pno_width)[None, :] < pno_count[rows][:, None]).astype(jnp.float32)
    window = live_pno[:, :, None] * live_pno[:, None, :]
    integral = integral * window
    energies = pno_energy[rows]
    occ_sum = occ_energy[pair_occ[rows, 0]] + occ_energy[pair_occ[rows, 1]]
    denominator = energies[:, :, None] + energies[:, None, :] - occ_sum[:, None, None]
    integral, denominator, window = (integral, denominator, window)
    amplitude = -integral / denominator
    residual = jnp.zeros_like(amplitude)
    for iteration in range(ITERS):
        arrived_i = lax.all_to_all(
            select_rows(amplitude, incoming_i), "occi", split_axis=0, concat_axis=0, tiled=True
        )
        arrived_j = lax.all_to_all(
            select_rows(amplitude, incoming_j), "occj", split_axis=0, concat_axis=0, tiled=True
        )
        terms_i = apply_terms(
            coupi_correlation, arrived_i.reshape(-1, pno_width, pno_width)[position_i], coupi_fock
        )
        terms_j = apply_terms(
            coupj_correlation, arrived_j.reshape(-1, pno_width, pno_width)[position_j], coupj_fock
        )
        coupled = scatter_terms(target_rows_i, terms_i) + scatter_terms(target_rows_j, terms_j)
        residual = window * (integral + denominator * amplitude - coupled)
        amplitude = amplitude - residual / denominator
    return (amplitude, residual)


def solution(mesh):
    placed = (
        P(("occi", "occj"), None, None),
        P(("occi", "occj"), None, None),
        P(("occi", "occj"), None),
        P(("occi", "occj")),
        P(("occi", "occj"), None),
        P(),
        P(("occi", "occj"), None),
        P(("occi", "occj")),
        P(("occi", "occj")),
        P(("occi", "occj")),
        P(("occi", "occj"), None, None),
        P(("occi", "occj"), None),
        P(("occi", "occj")),
        P(("occi", "occj")),
        P(("occi", "occj")),
        P(("occi", "occj"), None, None),
    )
    return jax.shard_map(
        local,
        mesh=mesh,
        in_specs=placed,
        out_specs=(P(("occi", "occj"), None, None), P(("occi", "occj"), None, None)),
        check_vma=False,
    )
```

profile of v0, /device:TPU:1, one launch (start us, length us, event | category | flops | bytes accessed | tf_op | source)
XLA Modules:
  0.0 675.4 jit_solution(2596963287285954450)
XLA Ops:
  12.4 6.0 all-to-all-start
  18.5 7.8 %gather_fusion.3 = f32[64,256,128]{2,1,0:T(8,128)} fusion(f32[64,256,128]{2,1,0:T(8,128)} %param.19, s32[1024]{0:T(1024)S(1)} %pad_clamp_fusion.8), kind=kCustom, calls=%fused_computation.3 | custom fusion | bytes 16777472 | tf_op jit(solution)/shard_map/gather | solution.py:90
  34.1 7.9 %all-to-all-start.2 = ((s32[16,1,4]{2,1,0:T(1,128)}), s32[16,1,4]{2,1,0:T(1,128)S(1)}, u32[]{:S(2)}, u32[]{:S(2)}) async-start(s32[16,1,4]{2,1,0:T(1,128)} %bitcast.26), calls=%async_computation.2 | async-start | bytes 16384 | tf_op jit(solution)/shard_map/all_to_all | solution.py:77
  45.5 72.6 %all-gather.3.cloned.1.call-done = f32[16,512,256]{2,1,0:T(8,128)} async-done(((f32[1,512,256]{2,1,0:T(8,128)}), f32[16,512,256]{2,1,0:T(8,128)}) %all-gather.3.cloned.1.call-update) | async-done | bytes 8388624 | tf_op jit(solution)/shard_map/all_gather | solution.py:59
  118.1 230.9 %while.10 = (s32[]{:T(128)}, f32[8,8,128,128]{3,1,0,2:T(8,128)}, s32[8,8]{1,0:T(8,128)S(1)}, f32[16,512,256]{2,1,0:T(8,128)}, f32[8,8,256,128]{3,2,1,0:T(8,128)}...) while((s32[]{:T(128)}, f32[8,8,128,128]{3,1,0,2:T(8,128)}, s32[8,8]{1,0:T(8,128)S(1)}, ...), condition=%wide.region_1.2_spmd, body=%wide.region_0.1_spmd.sunk | while | flops 4026533888 | bytes 45623156 | solution.py:85
  118.1 6.2 gather_fusion
  124.3 8.3 %fusion.80 = f32[8,512,128]{1,2,0:T(8,128)} fusion(f32[8,512,256]{2,1,0:T(8,128)} %gather_fusion, f32[8,8,256,128]{3,2,1,0:T(8,128)} %get-tuple-element.137, s32[]{:T(128)} %get-tuple-element.125), kind=kOutput, calls=%fused_computation.22.clone.1 | convolution fusion | flops 1610612736 | bytes 7340544 | tf_op jit(solution)/shard_map/while/body/eval_jaxpr/gqv,gva->gqa/dot_general | solution.py:70
  132.6 5.0 gather_fusion.1
  137.6 6.0 fusion.81
  147.0 6.2 gather_fusion
  153.2 8.3 %fusion.80 = f32[8,512,128]{1,2,0:T(8,128)} fusion(f32[8,512,256]{2,1,0:T(8,128)} %gather_fusion, f32[8,8,256,128]{3,2,1,0:T(8,128)} %get-tuple-element.137, s32[]{:T(128)} %get-tuple-element.125), kind=kOutput, calls=%fused_computation.22.clone.1 | convolution fusion | flops 1610612736 | bytes 7340544 | tf_op jit(solution)/shard_map/while/body/eval_jaxpr/gqv,gva->gqa/dot_general | solution.py:70
  161.4 5.0 gather_fusion.1
  166.5 6.0 fusion.81
  175.8 6.2 gather_fusion
  182.0 8.3 %fusion.80 = f32[8,512,128]{1,2,0:T(8,128)} fusion(f32[8,512,256]{2,1,0:T(8,128)} %gather_fusion, f32[8,8,256,128]{3,2,1,0:T(8,128)} %get-tuple-element.137, s32[]{:T(128)} %get-tuple-element.125), kind=kOutput, calls=%fused_computation.22.clone.1 | convolution fusion | flops 1610612736 | bytes 7340544 | tf_op jit(solution)/shard_map/while/body/eval_jaxpr/gqv,gva->gqa/dot_general | solution.py:70
  190.3 5.0 gather_fusion.1
  195.3 6.0 fusion.81
  204.7 6.2 gather_fusion
  210.9 8.3 %fusion.80 = f32[8,512,128]{1,2,0:T(8,128)} fusion(f32[8,512,256]{2,1,0:T(8,128)} %gather_fusion, f32[8,8,256,128]{3,2,1,0:T(8,128)} %get-tuple-element.137, s32[]{:T(128)} %get-tuple-element.125), kind=kOutput, calls=%fused_computation.22.clone.1 | convolution fusion | flops 1610612736 | bytes 7340544 | tf_op jit(solution)/shard_map/while/body/eval_jaxpr/gqv,gva->gqa/dot_general | solution.py:70
  219.2 5.0 gather_fusion.1
  224.2 6.0 fusion.81
  233.6 6.2 gather_fusion
  239.8 8.3 %fusion.80 = f32[8,512,128]{1,2,0:T(8,128)} fusion(f32[8,512,256]{2,1,0:T(8,128)} %gather_fusion, f32[8,8,256,128]{3,2,1,0:T(8,128)} %get-tuple-element.137, s32[]{:T(128)} %get-tuple-element.125), kind=kOutput, calls=%fused_computation.22.clone.1 | convolution fusion | flops 1610612736 | bytes 7340544 | tf_op jit(solution)/shard_map/while/body/eval_jaxpr/gqv,gva->gqa/dot_general | solution.py:70
  248.0 5.0 gather_fusion.1
  253.1 6.0 fusion.81
  262.4 6.2 gather_fusion
  268.6 8.3 %fusion.80 = f32[8,512,128]{1,2,0:T(8,128)} fusion(f32[8,512,256]{2,1,0:T(8,128)} %gather_fusion, f32[8,8,256,128]{3,2,1,0:T(8,128)} %get-tuple-element.137, s32[]{:T(128)} %get-tuple-element.125), kind=kOutput, calls=%fused_computation.22.clone.1 | convolution fusion | flops 1610612736 | bytes 7340544 | tf_op jit(solution)/shard_map/while/body/eval_jaxpr/gqv,gva->gqa/dot_general | solution.py:70
  276.9 5.0 gather_fusion.1
  281.9 6.0 fusion.81
  291.3 6.2 gather_fusion
  297.5 8.3 %fusion.80 = f32[8,512,128]{1,2,0:T(8,128)} fusion(f32[8,512,256]{2,1,0:T(8,128)} %gather_fusion, f32[8,8,256,128]{3,2,1,0:T(8,128)} %get-tuple-element.137, s32[]{:T(128)} %get-tuple-element.125), kind=kOutput, calls=%fused_computation.22.clone.1 | convolution fusion | flops 1610612736 | bytes 7340544 | tf_op jit(solution)/shard_map/while/body/eval_jaxpr/gqv,gva->gqa/dot_general | solution.py:70
  305.8 5.0 gather_fusion.1
  310.8 6.0 fusion.81
  320.2 6.2 gather_fusion
  326.4 8.3 %fusion.80 = f32[8,512,128]{1,2,0:T(8,128)} fusion(f32[8,512,256]{2,1,0:T(8,128)} %gather_fusion, f32[8,8,256,128]{3,2,1,0:T(8,128)} %get-tuple-element.137, s32[]{:T(128)} %get-tuple-element.125), kind=kOutput, calls=%fused_computation.22.clone.1 | convolution fusion | flops 1610612736 | bytes 7340544 | tf_op jit(solution)/shard_map/while/body/eval_jaxpr/gqv,gva->gqa/dot_general | solution.py:70
  334.6 5.0 gather_fusion.1
  339.7 6.0 fusion.81
  363.4 5.1 all-to-all-start.1
  373.6 43.8 %all-to-all-done.1 = f32[8,8,128,128]{3,2,1,0:T(8,128)} async-done(((f32[8,8,128,128]{3,2,1,0:T(8,128)}), f32[8,8,128,128]{3,2,1,0:T(8,128)}, u32[]{:S(2)}, u32[]{:S(2)}) %all-to-all-start.1) | async-done | bytes 4194336 | tf_op jit(solution)/shard_map/all_to_all | solution.py:104
  417.4 5.0 all-to-all-start.3
  434.8 5.3 fusion.19
  440.1 44.1 %all-to-all-done.3 = f32[16,4,128,128]{3,2,1,0:T(8,128)} async-done(((f32[16,4,128,128]{3,2,1,0:T(8,128)}), f32[16,4,128,128]{3,2,1,0:T(8,128)}, u32[]{:S(2)}, u32[]{:S(2)}) %all-to-all-start.3) | async-done | bytes 4194336 | tf_op jit(solution)/shard_map/all_to_all | solution.py:107
  497.6 7.6 %fusion.13 = f32[64,128,128]{2,0,1:T(8,128)S(1)} fusion(f32[64,128,128]{2,0,1:T(8,128)S(1)} %copy-done.8, f32[8,8,128,128]{3,1,0,2:T(8,128)} %get-tuple-element.39, f32[32,128,128]{2,1,0:T(8,128)S(1)} %convolution_multiply_fusion.2, f32[64]{0:T(128)S(1)} %add.146, f32[64,128]{1,0:T(8,128)S(1)} %gather_fusion.6, f32[64,128]{0,1:T(8,128)S(1)} %copy.59, ...), kind=kOutput, calls=%fused_computation.43 | convolution fusion | flops 416286720 | bytes 14811520 | tf_op jit(solution)/shard_map/cp,cab->pab/dot_general | solution.py:33
  516.6 6.5 all-to-all-start.4
  528.0 44.0 %all-to-all-done.4 = f32[8,8,128,128]{3,2,1,0:T(8,128)} async-done(((f32[8,8,128,128]{3,2,1,0:T(8,128)}), f32[8,8,128,128]{3,2,1,0:T(8,128)}, u32[]{:S(2)}, u32[]{:S(2)}) %all-to-all-start.4) | async-done | bytes 4194336 | tf_op jit(solution)/shard_map/all_to_all | solution.py:104
  588.9 5.2 fusion.16
  594.1 44.6 %all-to-all-done.5 = f32[16,4,128,128]{3,2,1,0:T(8,128)} async-done(((f32[16,4,128,128]{3,2,1,0:T(8,128)}), f32[16,4,128,128]{3,2,1,0:T(8,128)}, u32[]{:S(2)}, u32[]{:S(2)}) %all-to-all-start.5) | async-done | bytes 4194336 | tf_op jit(solution)/shard_map/all_to_all | solution.py:107
  652.1 7.4 %divide_subtract_fusion = (f32[64,128,128]{2,0,1:T(8,128)S(1)}, f32[64,128,128]{2,0,1:T(8,128)S(1)}) fusion(f32[64,128,128]{2,0,1:T(8,128)S(1)} %copy-done.10, f32[64]{0:T(128)S(1)} %add.146, f32[64,128]{1,0:T(8,128)S(1)} %gather_fusion.6, f32[64,128]{0,1:T(8,128)S(1)} %copy.59, f32[64,128,128]{2,0,1:T(8,128)S(1)} %copy-done.7, ...), kind=kOutput, calls=%fused_computation.44 | convolution fusion | flops 414189568 | bytes 23200128 | tf_op jit(solution)/shard_map/cp,cab->pab/dot_general | solution.py:33
  (169 shorter events, 144.0 us)
Async XLA Ops:
  7.2 419.5 %copy-start = (f32[32,128,128]{2,1,0:T(8,128)S(1)}, f32[32,128,128]{2,1,0:T(8,128)}, u32[]{:S(2)}) copy-start(f32[32,128,128]{2,1,0:T(8,128)} %param.28) | copy-start | bytes 6291460
  7.2 38.3 %all-gather.5.cloned.1.call-start = ((), (), s32[]{:S(2)}) async-start(), calls=%async_computation.7 | async-start | bytes 4718592 | tf_op jit(solution)/shard_map/all_gather | solution.py:60
  7.9 110.2 %all-gather.3.cloned.1.call-start = ((), (), s32[]{:S(2)}) async-start(), calls=%async_computation.6 | async-start | bytes 8912896 | tf_op jit(solution)/shard_map/all_gather | solution.py:59
  12.4 21.8 %all-to-all-start = ((s32[8,1,8]{2,1,0:T(1,128)}), s32[8,1,8]{2,1,0:T(1,128)S(1)}, u32[]{:S(2)}, u32[]{:S(2)}) async-start(s32[8,1,8]{2,1,0:T(1,128)} %bitcast.18), calls=%async_computation | async-start | bytes 8192 | tf_op jit(solution)/shard_map/all_to_all | solution.py:76
  18.4 7.8 %copy-start.2 = (s32[64,2]{0,1:T(2,128)S(1)}, s32[64,2]{0,1:T(2,128)}, u32[]{:S(2)}) copy-start(s32[64,2]{0,1:T(2,128)} %param.20) | copy-start | bytes 1540
  18.4 9.6 %copy-start.3 = (s32[64]{0:T(128)S(1)}, s32[64]{0:T(128)}, u32[]{:S(2)}) copy-start(s32[64]{0:T(128)} %param.21) | copy-start | bytes 772
  18.4 10.5 %copy-start.12 = (f32[64,128]{1,0:T(8,128)S(1)}, f32[64,128]{1,0:T(8,128)}, u32[]{:S(2)}) copy-start(f32[64,128]{1,0:T(8,128)} %param.22) | copy-start | bytes 98308
  18.4 12.1 %copy-start.11 = (s32[64]{0:T(128)S(1)}, s32[64]{0:T(128)}, u32[]{:S(2)}) copy-start(s32[64]{0:T(128)} %constant.150) | copy-start | bytes 772
  18.4 13.0 %copy-start.13 = (s32[32,1]{0,1:T(1,128)S(1)}, s32[32,1]{0,1:T(1,128)}, u32[]{:S(2)}) copy-start(s32[32,1]{0,1:T(1,128)} %param.29) | copy-start | bytes 388
  18.4 13.3 %copy-start.17 = (s32[32]{0:T(128)S(1)}, s32[32]{0:T(128)}, u32[]{:S(2)}) copy-start(s32[32]{0:T(128)} %param.30) | copy-start | bytes 388
  18.4 13.4 %copy-start.1 = (f32[128]{0:T(128)S(1)}, f32[128]{0:T(128)}, u32[]{:S(2)}) copy-start(f32[128]{0:T(128)} %param.23) | copy-start | bytes 1540
  34.1 329.2 %all-to-all-start.2 = ((s32[16,1,4]{2,1,0:T(1,128)}), s32[16,1,4]{2,1,0:T(1,128)S(1)}, u32[]{:S(2)}, u32[]{:S(2)}) async-start(s32[16,1,4]{2,1,0:T(1,128)} %bitcast.26), calls=%async_computation.2 | async-start | bytes 16384 | tf_op jit(solution)/shard_map/all_to_all | solution.py:77
  137.6 6.0 copy-start.4
  166.5 6.0 copy-start.4
  195.3 6.0 copy-start.4
  224.2 6.0 copy-start.4
  253.1 6.0 copy-start.4
  281.9 6.0 copy-start.4
  310.8 6.0 copy-start.4
  339.7 6.0 copy-start.4
  363.4 54.0 %all-to-all-start.1 = ((f32[8,8,128,128]{3,2,1,0:T(8,128)}), f32[8,8,128,128]{3,2,1,0:T(8,128)}, u32[]{:S(2)}, u32[]{:S(2)}) async-start(f32[8,8,128,128]{3,2,1,0:T(8,128)} %bitcast.135), calls=%async_computation.1 | async-start | bytes 8388608 | tf_op jit(solution)/shard_map/all_to_all | solution.py:104
  417.4 66.8 %all-to-all-start.3 = ((f32[16,4,128,128]{3,2,1,0:T(8,128)}), f32[16,4,128,128]{3,2,1,0:T(8,128)}, u32[]{:S(2)}, u32[]{:S(2)}) async-start(f32[16,4,128,128]{3,2,1,0:T(8,128)} %bitcast.133), calls=%async_computation.3 | async-start | bytes 8388608 | tf_op jit(solution)/shard_map/all_to_all | solution.py:107
  426.7 3.7 copy-start.14
  430.3 4.5 copy-start.15
  488.4 4.4 copy-start.5
  488.4 4.4 copy-start.16
  492.9 4.7 copy-start.8
  492.9 4.7 copy-start.18
  505.2 2.0 copy-start.9
  516.6 55.4 %all-to-all-start.4 = ((f32[8,8,128,128]{3,2,1,0:T(8,128)}), f32[8,8,128,128]{3,2,1,0:T(8,128)}, u32[]{:S(2)}, u32[]{:S(2)}) async-start(f32[8,8,128,128]{3,2,1,0:T(8,128)} %bitcast.136), calls=%async_computation.4 | async-start | bytes 8388608 | tf_op jit(solution)/shard_map/all_to_all | solution.py:104
  572.0 66.7 %all-to-all-start.5 = ((f32[16,4,128,128]{3,2,1,0:T(8,128)}), f32[16,4,128,128]{3,2,1,0:T(8,128)}, u32[]{:S(2)}, u32[]{:S(2)}) async-start(f32[16,4,128,128]{3,2,1,0:T(8,128)} %bitcast.134), calls=%async_computation.5 | async-start | bytes 8388608 | tf_op jit(solution)/shard_map/all_to_all | solution.py:107
  642.9 4.4 copy-start.6
  642.9 9.1 %copy-start.10 = (f32[64,128,128]{2,0,1:T(8,128)S(1)}, f32[64,128,128]{2,0,1:T(8,128)}, u32[]{:S(2)}) copy-start(f32[64,128,128]{2,0,1:T(8,128)} %copy-done.9) | copy-start | bytes 12582916
  647.4 4.7 copy-start.7
Sparse Core Ops, SparseCore 0:
  9.7 35.7 all-gather.4
  47.7 70.3 all-gather.2
where the time goes:
time: 680 us; the launch traced here: 675 us
  waiting for transfers between devices  254 us (37%)
  matrix products  192 us (28%)
  local copies, waits for them, and re-layouts  171 us (25%)
  starting transfers between devices  35.2 us (5%)
  between operations  14.7 us (2%)
  other arithmetic  8.72 us (1%)
    all_to_all x2, waiting for transfers between devices, local(): lax.all_to_all(select_rows(amplitude, incoming_j), 'occj', split_axis=0,...  88.8 us
    all_to_all x2, waiting for transfers between devices, local(): lax.all_to_all(select_rows(amplitude, incoming_i), 'occi', split_axis=0,...  87.8 us
    all_gather x1, waiting for transfers between devices, local(): block_first = lax.all_gather(factors, 'occj', axis=0, tiled=True)  72.6 us
    dot_general x8, matrix products, integrals(): jnp.einsum('gqv,gva->gqa', left_factor, vectors, precision=highest)  66.1 us
    gather x8, local copies, waits for them, and re-layouts, integrals(): left_factor = block_first[rows_first]  49.7 us
    dot_general x8, matrix products, integrals(): jnp.einsum('gqv,gva->gqa', right_factor, vectors, precision=highest)  47.7 us
    gather x8, local copies, waits for them, and re-layouts, integrals(): right_factor = block_second[rows_second]  40.1 us
    dot_general x4, matrix products, scatter_terms(): jnp.einsum('cp,cab->pab', target_rows, coupling_terms, precision=lax.Prec...  25.5 us
  transfers between devices with their start and end apart: 8, of which 6 were waited for; matrix products, arithmetic and copies ran while one was open for 46% of the time, Pallas kernels for 0%

commit v1 on v0

v1 whole, which is shorter than its diff:
```python
import functools

import jax
import jax.numpy as jnp
from jax import lax
from jax.experimental import pallas as pl
from jax.experimental.pallas import tpu as pltpu
from jax.sharding import PartitionSpec as P

MESH = pl.DeviceIdType.MESH
f32 = jnp.float32
bf16 = jnp.bfloat16
NI, NJ = 8, 16
CAPI, CAPJ = 8, 4
NP = 64
NC = 64
WAVES = 2
ROWS = 512 // WAVES
VMEM_ALL = 60 * 2**20

OFF_I = [(2, 0), (2, 1), (1, 0), (3, 0), (1, 1), (3, 1), (0, 1)]
OFF_J = sorted(
    [(a, b) for a in range(4) for b in range(4) if (a, b) != (0, 0)],
    key=lambda t: -(min(t[0], 4 - t[0]) + min(t[1], 4 - t[1])),
)


def split(x):
    hi = x.astype(bf16)
    return hi, (x - hi.astype(f32)).astype(bf16)


def dot(a, b):
    return jnp.dot(a, b, preferred_element_type=f32)


def dot_t(a, b):
    return lax.dot_general(a, b, (((1,), (1,)), ((), ())), preferred_element_type=f32)


def peer_i(u, off):
    return ((u // 2 + off[0]) % 4) * 2 + (u % 2 + off[1]) % 2


def peer_j(v, off):
    return ((v // 4 + off[0]) % 4) * 4 + (v % 4 + off[1]) % 4


def back(off, sizes):
    return tuple((n - o) % n for o, n in zip(off, sizes))


def greet(u, v):
    barrier = pltpu.get_barrier_semaphore()
    for off in OFF_I:
        pl.semaphore_signal(barrier, inc=1, device_id={"occi": peer_i(u, off)}, device_id_type=MESH)
    for off in OFF_J:
        pl.semaphore_signal(barrier, inc=1, device_id={"occj": peer_j(v, off)}, device_id_type=MESH)
    pl.semaphore_wait(barrier, len(OFF_I) + len(OFF_J))


def tables_kernel(pi, si, ti, pj, sj, tj, ri, rj, src, order, same, last, ci, cj, cnt):
    ri[...] = jnp.zeros_like(ri)
    rj[...] = jnp.zeros_like(rj)

    def zero(k, c):
        cnt[k] = 0
        return c

    lax.fori_loop(0, NP + 1, zero, 0)
    for k in range(NI):
        ci[k] = 0
    for k in range(NJ):
        cj[k] = 0

    def place_i(c, carry):
        p = pi[c]
        k = ci[p]
        ci[p] = k + 1
        ri[p, pl.ds(k, 1), :] = jnp.full((1, 128), si[c], jnp.int32)
        src[c] = p * CAPI + k
        t = ti[c]
        cnt[t + 1] = cnt[t + 1] + 1
        return carry

    def place_j(c, carry):
        p = pj[c]
        k = cj[p]
        cj[p] = k + 1
        rj[p, pl.ds(k, 1), :] = jnp.full((1, 128), sj[c], jnp.int32)
        src[32 + c] = NI * CAPI + p * CAPJ + k
        t = tj[c]
        cnt[t + 1] = cnt[t + 1] + 1
        return carry

    lax.fori_loop(0, 32, place_i, 0)
    lax.fori_loop(0, 32, place_j, 0)

    def prefix(p, carry):
        n = cnt[p + 1]
        cnt[p + 1] = carry + n
        last[p] = jnp.where(n > 0, carry + n - 1, NC)
        return carry + n

    lax.fori_loop(0, NP, prefix, 0)

    def sort(t, c):
        s = cnt[t]
        cnt[t] = s + 1
        order[s] = c
        same[s] = jnp.where(last[t] == s, 1, 0)

    def sort_i(c, carry):
        sort(ti[c], c)
        return carry

    def sort_j(c, carry):
        sort(tj[c], c + 32)
        return carry

    lax.fori_loop(0, 32, sort_i, 0)
    lax.fori_loop(0, 32, sort_j, 0)

    def shift(k, carry):
        s = NC - 1 - k
        before = same[jnp.maximum(s - 1, 0)]
        same[s] = jnp.where(s == 0, 0, 1 - before)
        return carry

    lax.fori_loop(0, NC, shift, 0)


def tables(pi, si, ti, pj, sj, tj):
    smem = pl.BlockSpec(memory_space=pltpu.SMEM)
    vmem = pl.BlockSpec(memory_space=pltpu.VMEM)
    i32 = jnp.int32
    return pl.pallas_call(
        tables_kernel,
        out_shape=(
            jax.ShapeDtypeStruct((NI, 8, 128), i32),
            jax.ShapeDtypeStruct((NJ, 8, 128), i32),
            jax.ShapeDtypeStruct((NC,), i32),
            jax.ShapeDtypeStruct((NC,), i32),
            jax.ShapeDtypeStruct((NC,), i32),
            jax.ShapeDtypeStruct((NP,), i32),
        ),
        in_specs=[smem] * 6,
        out_specs=(vmem, vmem, smem, smem, smem, smem),
        scratch_shapes=[pltpu.SMEM((NI,), i32), pltpu.SMEM((NJ,), i32), pltpu.SMEM((NP + 1,), i32)],
    )(pi, si, ti, pj, sj, tj)


def gather_kernel(fac, ri, rj, fi, fj, qi, qj, own_sem, tab_sem, rs, ss, crs, css):
    u = lax.axis_index("occi")
    v = lax.axis_index("occj")
    x, z = v % 4, v // 4
    y, core = u // 2, u % 2

    def vid(zz, xx):
        return ((z + zz) % 4) * 4 + (x + xx) % 4

    def uid(yy, cc):
        return ((y + yy) % 4) * 2 + (core + cc) % 2

    greet(u, v)
    pending = []

    own = [
        pltpu.make_async_copy(fac.at[0], fi.at[v], own_sem.at[0]),
        pltpu.make_async_copy(fac.at[0], fj.at[u], own_sem.at[1]),
        pltpu.make_async_copy(ri.at[u], qi.at[u], own_sem.at[2]),
        pltpu.make_async_copy(rj.at[v], qj.at[v], own_sem.at[3]),
    ]
    for c in own:
        c.start()
    waits = []
    for k, off in enumerate(OFF_I):
        to, frm = peer_i(u, off), peer_i(u, back(off, (4, 2)))
        c = pltpu.make_async_remote_copy(ri.at[to], qi.at[u], tab_sem.at[0, k], tab_sem.at[1, k], {"occi": to}, MESH)
        c.start()
        pending.append(c)
        waits.append(pltpu.make_async_remote_copy(ri.at[frm], qi.at[frm], tab_sem.at[0, k], tab_sem.at[1, k], {"occi": to}, MESH))
    for k, off in enumerate(OFF_J):
        to, frm = peer_j(v, off), peer_j(v, back(off, (4, 4)))
        c = pltpu.make_async_remote_copy(rj.at[to], qj.at[v], tab_sem.at[0, 7 + k], tab_sem.at[1, 7 + k], {"occj": to}, MESH)
        c.start()
        pending.append(c)
        waits.append(pltpu.make_async_remote_copy(rj.at[frm], qj.at[frm], tab_sem.at[0, 7 + k], tab_sem.at[1, 7 + k], {"occj": to}, MESH))

    def send(src, buf, slot, q, n, sem, dev):
        at = buf.at[slot, pl.ds(q, n)]
        c = pltpu.make_async_remote_copy(at if src is None else src.at[0, pl.ds(q, n)], at, sem[0], sem[1], dev, MESH)
        c.start()
        pending.append(c)

    def got(buf, slot, q, n, sem, dev):
        at = buf.at[slot, pl.ds(q, n)]
        pltpu.make_async_remote_copy(at, at, sem[0], sem[1], dev, MESH).wait_recv()

    def wave(w):
        h = ROWS // 2
        s = h // 2

        def sem(half, k):
            return ss.at[w, half, k], rs.at[w, half, k]

        halves = []
        for half in (0, 1):
            q = w * ROWS + half * h
            if half == 0:
                first = lambda d: {"occj": vid(0, d)}
                second = lambda d: {"occj": vid(d, 0)}
                slot = lambda a, b: vid(b, a)
            else:
                first = lambda d: {"occj": vid(d, 0)}
                second = lambda d: {"occj": vid(0, d)}
                slot = lambda a, b: vid(a, b)
            halves.append((half, q, first, second, slot))

        def second_send(half, q, second, slot, a, base, src=None):
            send(src, fi, slot(a, 0), q, h, sem(half, base), second(1))
            send(src, fi, slot(a, 0), q, h, sem(half, base + 1), second(3))

        def second_forward(half, q, second, slot, a, base):
            got(fi, slot(a, 3), q, h, sem(half, base), second(1))
            send(None, fi, slot(a, 3), q, s, sem(half, base + 2), second(1))
            got(fi, slot(a, 1), q, h, sem(half, base + 1), second(1))
            send(None, fi, slot(a, 1), q + s, s, sem(half, base + 3), second(3))

        def s0():
            for half, q, first, second, slot in halves:
                send(fac, fi, v, q, h, sem(half, 0), first(1))
                send(fac, fi, v, q, h, sem(half, 1), first(3))
            for half, q, first, second, slot in halves:
                second_send(half, q, second, slot, 0, 4, fac)
            q = w * ROWS
            send(fac, fj, u, q, ROWS, (css.at[w, 0], crs.at[w, 0]), {"occi": uid(1, 0)})
            send(fac, fj, u, q, ROWS, (css.at[w, 1], crs.at[w, 1]), {"occi": uid(3, 0)})
            send(fac, fj, u, q, ROWS, (css.at[w, 4], crs.at[w, 4]), {"occi": uid(0, 1)})

        def s1():
            for half, q, first, second, slot in halves:
                got(fi, slot(3, 0), q, h, sem(half, 0), first(1))
                send(None, fi, slot(3, 0), q, s, sem(half, 2), first(1))
                got(fi, slot(1, 0), q, h, sem(half, 1), first(1))
                send(None, fi, slot(1, 0), q + s, s, sem(half, 3), first(3))
            for half, q, first, second, slot in halves:
                second_send(half, q, second, slot, 3, 8)
                second_send(half, q, second, slot, 1, 12)

        def s2():
            for half, q, first, second, slot in halves:
                second_forward(half, q, second, slot, 0, 4)
            q, n = w * ROWS, ROWS // 2
            got(fj, uid(3, 0), q, ROWS, (css.at[w, 0], crs.at[w, 0]), {"occi": uid(1, 0)})
            send(None, fj, uid(3, 0), q, n, (css.at[w, 2], crs.at[w, 2]), {"occi": uid(1, 0)})
            send(None, fj, uid(3, 0), q, ROWS, (css.at[w, 5], crs.at[w, 5]), {"occi": uid(0, 1)})
            got(fj, uid(1, 0), q, ROWS, (css.at[w, 1], crs.at[w, 1]), {"occi": uid(1, 0)})
            send(None, fj, uid(1, 0), q + n, n, (css.at[w, 3], crs.at[w, 3]), {"occi": uid(3, 0)})
            send(None, fj, uid(1, 0), q, ROWS, (css.at[w, 6], crs.at[w, 6]), {"occi": uid(0, 1)})

        def s3():
            for half, q, first, second, slot in halves:
                got(fi, slot(2, 0), q, s, sem(half, 2), first(1))
                got(fi, slot(2, 0), q + s, s, sem(half, 3), first(1))
                second_send(half, q, second, slot, 2, 16)

        def s4():
            for half, q, first, second, slot in halves:
                second_forward(half, q, second, slot, 3, 8)
                second_forward(half, q, second, slot, 1, 12)
            q, n = w * ROWS, ROWS // 2
            got(fj, uid(2, 0), q, n, (css.at[w, 2], crs.at[w, 2]), {"occi": uid(1, 0)})
            got(fj, uid(2, 0), q + n, n, (css.at[w, 3], crs.at[w, 3]), {"occi": uid(1, 0)})
            send(None, fj, uid(2, 0), q, ROWS, (css.at[w, 7], crs.at[w, 7]), {"occi": uid(0, 1)})

        def s5():
            for half, q, first, second, slot in halves:
                second_forward(half, q, second, slot, 2, 16)

        def s6():
            for half, q, first, second, slot in halves:
                for a, base in ((0, 4), (3, 8), (1, 12), (2, 16)):
                    got(fi, slot(a, 2), q, s, sem(half, base + 2), second(1))
                    got(fi, slot(a, 2), q + s, s, sem(half, base + 3), second(1))
            q = w * ROWS
            for k, yy in ((4, 0), (5, 3), (6, 1), (7, 2)):
                got(fj, uid(yy, 1), q, ROWS, (css.at[w, k], crs.at[w, k]), {"occi": uid(0, 1)})

        return s0, s1, s2, s3, s4, s5, s6

    a, b = wave(0), wave(1)
    for step in (a[0], a[1], b[0], a[2], a[3], b[1], a[4], b[2], a[5], b[3], b[4], a[6], b[5], b[6]):
        step()
    for c in waits:
        c.wait_recv()
    for c in pending:
        c.wait_send()
    for c in own:
        c.wait()


def gather(factors, ri, rj):
    anyw = pl.BlockSpec(memory_space=pl.ANY)
    i32 = jnp.int32
    dma = pltpu.SemaphoreType.DMA
    return pl.pallas_call(
        gather_kernel,
        out_shape=(
            jax.ShapeDtypeStruct((NJ, 512, 256), f32),
            jax.ShapeDtypeStruct((NI, 512, 256), f32),
            jax.ShapeDtypeStruct((NI, 8, 128), i32),
            jax.ShapeDtypeStruct((NJ, 8, 128), i32),
        ),
        in_specs=[anyw] * 3,
        out_specs=(anyw,) * 4,
        scratch_shapes=[
            dma((4,)),
            dma((2, 22)),
            dma((WAVES, 2, 20)),
            dma((WAVES, 2, 20)),
            dma((WAVES, 8)),
            dma((WAVES, 8)),
        ],
        compiler_params=pltpu.CompilerParams(collective_id=0, has_side_effects=True, vmem_limit_bytes=VMEM_ALL),
    )(factors, ri, rj)


GROUP = 4


def integral_kernel(occ, cnt, eo, fi, fj, v_ref, en, amp, inv, th, tl, jh, jl):
    step = pl.program_id(0)
    u = lax.axis_index("occi")

    @pl.when(step == 0)
    def _():
        def bi(k, c):
            h, l = split(jnp.transpose(fi[k]))
            th[k] = h
            tl[k] = l
            return c

        def bj(k, c):
            h, l = split(fj[k])
            jh[k] = h
            jl[k] = l
            return c

        lax.fori_loop(0, NJ, bi, 0)
        lax.fori_loop(0, NI, bj, 0)

    rows = lax.broadcasted_iota(jnp.int32, (128, 128), 0)
    cols = lax.broadcasted_iota(jnp.int32, (128, 128), 1)

    for g in range(GROUP):
        p = step * GROUP + g
        oi, oj = occ[0, p], occ[1, p]
        i, j = oi - u * NJ, oj // NJ
        vec = v_ref[g]
        vh, vl = split(vec)
        vth, vtl = split(jnp.transpose(vec))
        t2 = dot(jnp.concatenate([vth, vtl], axis=0), th[i])
        lt = t2[:128] + t2[128:] + dot(vth, tl[i])
        r2 = dot(jh[j], jnp.concatenate([vh, vl], axis=1))
        r = r2[:, :128] + r2[:, 128:] + dot(jl[j], vh)
        lh, ll = split(lt)
        rh, rl = split(r)
        o = dot(jnp.concatenate([lh, ll], axis=0), jnp.concatenate([rh, rl], axis=1))
        o = (o[:128, :128] + o[:128, 128:]) + o[128:, :128]
        across = jnp.broadcast_to(en[pl.ds(g, 1), :] if False else en[0, pl.ds(g, 1), :], (128, 128))
        den = jnp.transpose(across) + across - (eo[oi] + eo[oj])
        n = cnt[p]
        m = jnp.where((rows < n) & (cols < n), 1.0 / den, 0.0)
        inv[g] = m
        amp[g] = -o * m


def integrals(occ, cnt, eo, fi, fj, vecs, en):
    smem = pl.BlockSpec(memory_space=pltpu.SMEM)
    vmem = pl.BlockSpec(memory_space=pltpu.VMEM)
    block = pl.BlockSpec((GROUP, 128, 128), lambda s: (s, 0, 0))
    return pl.pallas_call(
        integral_kernel,
        grid=(NP // GROUP,),
        out_shape=(jax.ShapeDtypeStruct((NP, 128, 128), f32),) * 2,
        in_specs=[
            smem,
            smem,
            smem,
            vmem,
            vmem,
            pl.BlockSpec((GROUP, 256, 128), lambda s: (s, 0, 0)),
            pl.BlockSpec((1, GROUP, 128), lambda s: (s, 0, 0)),
        ],
        out_specs=(block, block),
        scratch_shapes=[pltpu.VMEM((NJ, 256, 512), bf16)] * 2 + [pltpu.VMEM((NI, 512, 256), bf16)] * 2,
        compiler_params=pltpu.CompilerParams(vmem_limit_bytes=VMEM_ALL),
    )(occ, cnt, eo, fi, fj, vecs, en.reshape(NP // GROUP, GROUP, 128))


UNROLL = 4
SEND = 7 * CAPI + 15 * CAPJ


def iterate_kernel(
    qi, qj, src, order, same, last, fock, cnt, amp0, inv0, ci, cj, amp_out, res_out,
    amp, inv, corr, delta, term, snd, rcv0, rcv1, ls, ss, rs,
):
    u = lax.axis_index("occi")
    v = lax.axis_index("occj")
    arrived = (rcv0, rcv1)
    loads = [
        pltpu.make_async_copy(amp0, amp, ls.at[0]),
        pltpu.make_async_copy(inv0, inv, ls.at[1]),
        pltpu.make_async_copy(ci, corr.at[pl.ds(0, 32)], ls.at[2]),
        pltpu.make_async_copy(cj, corr.at[pl.ds(32, 32)], ls.at[3]),
    ]
    for c in loads:
        c.start()
    greet(u, v)
    term[NC] = jnp.zeros((128, 128), f32)

    def exchange(it, x):
        copies, waits = [], []
        at_i, at_j = 0, 7 * CAPI
        jobs = []
        for k in range(15):
            if k < 7:
                jobs.append((0, k))
            jobs.append((1, k))
        for axis, k in jobs:
            if axis == 0:
                off, cap, q, name, base = OFF_I[k], CAPI, qi, "occi", k * CAPI
                to, frm, mine = peer_i(u, off), peer_i(u, back(off, (4, 2))), u * CAPI
                came, sem = frm * CAPI, k
            else:
                off, cap, q, name, base = OFF_J[k], CAPJ, qj, "occj", 7 * CAPI + k * CAPJ
                to, frm, mine = peer_j(v, off), peer_j(v, back(off, (4, 4))), NI * CAPI + v * CAPJ
                came, sem = NI * CAPI + frm * CAPJ, 7 + k
            for s in range(cap):
                snd[base + s] = x[q[to, s]]
            c = pltpu.make_async_remote_copy(
                snd.at[pl.ds(base, cap)], arrived[it].at[pl.ds(mine, cap)], ss.at[it, sem], rs.at[it, sem], {name: to}, MESH
            )
            c.start()
            copies.append(c)
            waits.append(
                pltpu.make_async_remote_copy(
                    snd.at[pl.ds(base, cap)], arrived[it].at[pl.ds(came, cap)], ss.at[it, sem], rs.at[it, sem], {name: to}, MESH
                )
            )
        for s in range(CAPI):
            arrived[it][u * CAPI + s] = x[qi[u, s]]
        for s in range(CAPJ):
            arrived[it][NI * CAPI + v * CAPJ + s] = x[qj[v, s]]
        return copies, waits

    def couple(it):
        def body(b, run):
            for k in range(UNROLL):
                s = b * UNROLL + k
                c = order[s]
                m = corr[c]
                mh, ml = split(m)
                xh, xl = split(arrived[it][src[c]])
                xx = jnp.concatenate([xh, xl], axis=1)
                h = dot(jnp.concatenate([mh, ml], axis=1), jnp.concatenate([xx, xx], axis=0))
                hh, hl = split(h[:, :128] + h[:, 128:])
                m4 = jnp.concatenate([jnp.concatenate([mh, mh], axis=1), jnp.concatenate([ml, ml], axis=1)], axis=0)
                t = dot_t(jnp.concatenate([hh, hl], axis=1), m4)
                t = (t[:, :128] + t[:, 128:]) * fock[c]
                run = jnp.where(same[s] > 0, run, 0.0) + t
                term[s] = run
            return run

        lax.fori_loop(0, NC // UNROLL, body, jnp.zeros((128, 128), f32))

    for c in loads:
        c.wait()
    copies, waits = exchange(0, amp)
    for c in waits:
        c.wait_recv()
    for c in copies:
        c.wait_send()
    couple(0)

    def first(p, carry):
        delta[p] = term[last[p]] * inv[p]
        return carry

    lax.fori_loop(0, NP, first, 0)
    copies, waits = exchange(1, delta)
    for c in waits:
        c.wait_recv()
    for c in copies:
        c.wait_send()
    couple(1)
    rows = lax.broadcasted_iota(jnp.int32, (128, 128), 0)
    cols = lax.broadcasted_iota(jnp.int32, (128, 128), 1)

    def second(p, carry):
        s = term[last[p]]
        n = cnt[p]
        amp[p] = amp[p] + delta[p] + s * inv[p]
        inv[p] = jnp.where((rows < n) & (cols < n), -s, 0.0)
        return carry

    lax.fori_loop(0, NP, second, 0)
    outs = [pltpu.make_async_copy(amp, amp_out, ls.at[0]), pltpu.make_async_copy(inv, res_out, ls.at[1])]
    for c in outs:
        c.start()
    for c in outs:
        c.wait()


def iterate(qi, qj, src, order, same, last, fock, cnt, amp, inv, ci, cj):
    smem = pl.BlockSpec(memory_space=pltpu.SMEM)
    anyw = pl.BlockSpec(memory_space=pl.ANY)
    dma = pltpu.SemaphoreType.DMA
    mats = lambda n: pltpu.VMEM((n, 128, 128), f32)
    return pl.pallas_call(
        iterate_kernel,
        out_shape=(jax.ShapeDtypeStruct((NP, 128, 128), f32),) * 2,
        in_specs=[smem] * 8 + [anyw] * 4,
        out_specs=(anyw, anyw),
        scratch_shapes=[
            mats(NP),
            mats(NP),
            mats(NC),
            mats(NP),
            mats(NC + 1),
            mats(SEND),
            mats(NI * CAPI + NJ * CAPJ),
            mats(NI * CAPI + NJ * CAPJ),
            dma((4,)),
            dma((2, 22)),
            dma((2, 22)),
        ],
        compiler_params=pltpu.CompilerParams(collective_id=1, has_side_effects=True, vmem_limit_bytes=VMEM_ALL),
    )(qi, qj, src, order, same, last, fock, cnt, amp, inv, ci, cj)


def local(
    factors, pno_vecs, pair_occ, pno_count, pno_energy, occ_energy,
    coupi_peer, coupi_slot, coupi_target, coupi_fock, coupi_correlation,
    coupj_peer, coupj_slot, coupj_target, coupj_fock, coupj_correlation,
):
    ri, rj, src, order, same, last = tables(
        coupi_peer[:, 0], coupi_slot, coupi_target, coupj_peer[:, 0], coupj_slot, coupj_target
    )
    fi, fj, qi, qj = gather(factors, ri, rj)
    amp, inv = integrals(pair_occ.T, pno_count, occ_energy, fi, fj, pno_vecs, pno_energy)
    fock = jnp.concatenate([coupi_fock, coupj_fock])
    return iterate(
        qi[:, :, 0], qj[:, :CAPJ, 0], src, order, same, last, fock, pno_count, amp, inv, coupi_correlation, coupj_correlation
    )


def solution(mesh):
    both = ("occi", "occj")
    three, two, one = P(both, None, None), P(both, None), P(both)
    placed = (
        three, three, two, one, two, P(),
        two, one, one, one, three,
        two, one, one, one, three,
    )
    return jax.shard_map(local, mesh=mesh, in_specs=placed, out_specs=(three, three), check_vma=False)
```

time: 680 us -> 248 us (0.36)
  waiting for transfers between devices: 254 us -> 0 us
  Pallas kernels: 0 us -> 235 us
  matrix products: 192 us -> 0 us
  local copies, waits for them, and re-layouts: 171 us -> 10.1 us
  starting transfers between devices: 35.2 us -> 0 us
  between operations: 14.7 us -> 0.67 us
  other arithmetic: 8.72 us -> 1.26 us
    pallas_call x0 -> x4, Pallas kernels: none -> 235 us  [the longest x1 138 us: iterate(): pl.pallas_call(iterate_kernel, out_shape=(jax.ShapeDtypeStruct((NP, 128,...]
    dot_general x36 -> x0, matrix products: 192 us -> none  [the longest x8 66.1 us: integrals(): jnp.einsum('gqv,gva->gqa', left_factor, vectors, precision=highest)]
    all_to_all x6 -> x0, waiting for transfers between devices: 177 us -> none  [the longest x2 88.8 us: local(): lax.all_to_all(select_rows(amplitude, incoming_j), 'occj', split_axis=0,...]
    gather x34 -> x0, local copies, waits for them, and re-layouts: 141 us -> none  [the longest x8 49.7 us: integrals(): left_factor = block_first[rows_first]]
    all_gather x2 -> x0, waiting for transfers between devices: 75.9 us -> none  [the longest x1 72.6 us: local(): block_first = lax.all_gather(factors, 'occj', axis=0, tiled=True)]
    all_to_all x6 -> x0, starting transfers between devices: 35.1 us -> none  [the longest x2 11.6 us: local(): lax.all_to_all(select_rows(amplitude, incoming_i), 'occi', split_axis=0,...]
    dynamic_update_slice x8 -> x0, local copies, waits for them, and re-layouts: 8.85 us -> none  [local(): lax.map(integrals, (local_first[padded_rows].reshape(group_count, 8), loc...]
  transfers between devices with their start and end apart: 8 -> 0, of which waited for: 6 -> 0; matrix products, arithmetic and copies ran while one was open for 46% -> 0% of each run, Pallas kernels for 0% -> 0%
where the time goes in v1:
time: 248 us; the launch traced here: 247 us
  Pallas kernels  235 us (95%)
  local copies, waits for them, and re-layouts  10.1 us (4%)
    pallas_call x1, Pallas kernels, iterate(): pl.pallas_call(iterate_kernel, out_shape=(jax.ShapeDtypeStruct((NP, 128,...  138 us
    pallas_call x1, Pallas kernels, gather(): pl.pallas_call(gather_kernel, out_shape=(jax.ShapeDtypeStruct((NJ, 512, 2...  55 us
    pallas_call x1, Pallas kernels, integrals(): pl.pallas_call(integral_kernel, grid=(NP // GROUP,), out_shape=(jax.Shape...  38.5 us
    unnamed x4, local copies, waits for them, and re-layouts  6.87 us

profile of v1, /device:TPU:1, one launch (start us, length us, event | category | flops | bytes accessed | tf_op | source)
XLA Modules:
  0.0 247.0 jit_solution(3470235000977673061)
XLA Ops:
  0.6 1.3 pad_maximum_fusion.fock
  1.9 4.0 %shard_map.167 = (s32[8,8,128]{2,1,0:T(8,128)}, s32[16,8,128]{2,1,0:T(8,128)}, s32[64]{0:T(128)}, s32[64]{0:T(128)}, s32[64]{0:T(128)}, /*index=5*/s32[64]{0:T(128)}) custom-call(s32[32]{0:T(128)} %bitcast.8, s32[32]{0:T(128)} %si.1, s32[32]{0:T(128)} %ti.1, s32[32]{0:T(128)} %bitcast.9, s32[32]{0:T(128)} %sj.1, s32[32]{0:T(128)} %tj.1), custom_call_target="tpu_custom_call" | custom-call | tf_op jit(solution)/shard_map/pallas_call | solution.py:137
  5.9 55.0 %shard_map.168 = (f32[16,512,256]{2,1,0:T(8,128)}, f32[8,512,256]{2,1,0:T(8,128)}, s32[8,8,128]{2,1,0:T(8,128)}, s32[16,8,128]{2,1,0:T(8,128)}) custom-call(f32[1,512,256]{2,1,0:T(8,128)} %fac.1, s32[8,8,128]{2,1,0:T(8,128)} %get-tuple-element.14.ri, s32[16,8,128]{2,1,0:T(8,128)} %get-tuple-element.15.rj), custom_call_target="tpu_custom_call" | custom-call | tf_op jit(solution)/shard_map/pallas_call | solution.py:307
  60.9 1.6 slice_reduce_fusion.qi
  62.5 0.8 slice.7
  63.3 0.1 copy.20
  63.4 0.7 copy.21.qj
  64.1 38.5 %shard_map.169 = (f32[64,128,128]{2,1,0:T(8,128)}, f32[64,128,128]{2,1,0:T(8,128)}) custom-call(s32[2,64]{1,0:T(2,128)} %bitcast.7, s32[64]{0:T(128)} %cnt.3, f32[128]{0:T(128)} %eo.1, f32[16,512,256]{2,1,0:T(8,128)} %get-tuple-element.22.fi, f32[8,512,256]{2,1,0:T(8,128)} %get-tuple-element.23.fj, f32[64,256,128]{2,1,0:T(8,128)} %v_ref.1, f32[16,4,128]{2,1,0:T(4,128)} %bitcast.5), custom_call_target="tpu_custom_call" | custom-call | tf_op jit(solution)/shard_map/pallas_call | solution.py:383
  102.6 137.6 %shard_map.170 = (f32[64,128,128]{2,1,0:T(8,128)}, f32[64,128,128]{2,1,0:T(8,128)}) custom-call(s32[8,8]{1,0:T(8,128)} %slice_reduce_fusion.qi, s32[16,4]{1,0:T(8,128)} %copy.21.qj, s32[64]{0:T(128)} %get-tuple-element.18.src, s32[64]{0:T(128)} %get-tuple-element.19.order, s32[64]{0:T(128)} %get-tuple-element.20.same, s32[64]{0:T(128)} %get-tuple-element.21.last, ...), custom_call_target="tpu_custom_call" | custom-call | tf_op jit(solution)/shard_map/pallas_call | solution.py:522
  240.1 0.0 copy-start
  240.1 4.8 %copy.24 = f32[64,128,128]{2,1,0:T(8,128)} copy(f32[64,128,128]{2,1,0:T(8,128)} %get-tuple-element.28) | data formatting | bytes 8388608
  245.0 0.0 copy-done
  245.0 2.0 copy.25
Async XLA Ops:
  240.1 4.9 %copy-start = (f32[64,128,128]{2,1,0:T(8,128)S(1)}, f32[64,128,128]{2,1,0:T(8,128)}, u32[]{:S(2)}) copy-start(f32[64,128,128]{2,1,0:T(8,128)} %get-tuple-element.29) | copy-start | bytes 12582916

commit v2 on v0

v2 whole, which is shorter than its diff:
```python
import functools

import jax
import jax.numpy as jnp
from jax import lax
from jax.experimental import pallas as pl
from jax.experimental.pallas import tpu as pltpu
from jax.sharding import PartitionSpec as P

MESH = pl.DeviceIdType.MESH
f32 = jnp.float32
bf16 = jnp.bfloat16
NI, NJ = 8, 16
CAPI, CAPJ = 8, 4
NP = 64
NC = 64
WAVES = 2
ROWS = 512 // WAVES
VMEM_ALL = 60 * 2**20
GROUP = 4

OFF_I = [(2, 0), (2, 1), (1, 0), (3, 0), (1, 1), (3, 1), (0, 1)]
OFF_J = sorted(
    [(a, b) for a in range(4) for b in range(4) if (a, b) != (0, 0)],
    key=lambda t: -(min(t[0], 4 - t[0]) + min(t[1], 4 - t[1])),
)


def split(x):
    hi = x.astype(bf16)
    return hi, (x - hi.astype(f32)).astype(bf16)


def dot(a, b):
    return jnp.dot(a, b, preferred_element_type=f32)


def dot_t(a, b):
    return lax.dot_general(a, b, (((1,), (1,)), ((), ())), preferred_element_type=f32)


def peer_i(u, off):
    return ((u // 2 + off[0]) % 4) * 2 + (u % 2 + off[1]) % 2


def peer_j(v, off):
    return ((v // 4 + off[0]) % 4) * 4 + (v % 4 + off[1]) % 4


def back(off, sizes):
    return tuple((n - o) % n for o, n in zip(off, sizes))


def greet(u, v):
    barrier = pltpu.get_barrier_semaphore()
    for off in OFF_I:
        pl.semaphore_signal(barrier, inc=1, device_id={"occi": peer_i(u, off)}, device_id_type=MESH)
    for off in OFF_J:
        pl.semaphore_signal(barrier, inc=1, device_id={"occj": peer_j(v, off)}, device_id_type=MESH)
    pl.semaphore_wait(barrier, len(OFF_I) + len(OFF_J))


def tables(tab, ri, rj, plan, weight):
    lane = lax.broadcasted_iota(jnp.int32, (NC, 128), 1)
    sub = lax.broadcasted_iota(jnp.int32, (NC, 128), 0)

    def across(r):
        return jnp.broadcast_to(tab[pl.ds(r, 1), :], (128, 128))

    def down(r):
        return jnp.transpose(across(r))[:NC]

    def count(mask, axis):
        return jnp.sum(jnp.where(mask, 1.0, 0.0), axis=axis, keepdims=True)

    def pick(mask, value):
        return jnp.sum(jnp.where(mask, value, 0.0), axis=0, keepdims=True)

    peer, slot, target, fock = down(0), down(1), down(2), down(3)
    rank = count((across(0)[:NC] == peer) & (lane < sub), 1)
    at = rank.astype(jnp.int32)
    for p in range(NI):
        ri[p] = pick((peer == p) & (at == lane), slot).astype(jnp.int32)
    for p in range(NJ):
        rj[p] = pick((peer == NI + p) & (at == lane), slot).astype(jnp.int32)
    arrival = jnp.where(peer < NI, peer * CAPI, NI * CAPI + (peer - NI) * CAPJ) + rank
    row_t = across(2)[:NC]
    equal = row_t == target
    place = count((row_t < target) | (equal & (lane < sub)), 1).astype(jnp.int32)
    goes_on = jnp.minimum(count(equal & (lane < sub), 1), 1.0)
    here = place == lane
    plan[pl.ds(0, 1), :] = pick(here, sub.astype(f32)).astype(jnp.int32)
    plan[pl.ds(1, 1), :] = pick(here, arrival).astype(jnp.int32)
    plan[pl.ds(2, 1), :] = pick(here, goes_on).astype(jnp.int32)
    lane_f = lane.astype(f32)
    upto = count(target <= lane_f, 0)
    plan[pl.ds(3, 1), :] = jnp.where(count(target == lane_f, 0) > 0.5, upto - 1.0, float(NC)).astype(jnp.int32)
    weight[...] = pick(here, fock)


def integral_kernel(
    occ, cnt, eo, tab, en, fac, vecs, amp, qi, qj, plan, weight,
    fi0, fi1, fj0, fj1, th, tl, jh, jl, vec, acc, ri, rj, own_sem, tab_sem, rs, ss, crs, css, out_sem,
):
    u = lax.axis_index("occi")
    v = lax.axis_index("occj")
    x, z = v % 4, v // 4
    y, core = u // 2, u % 2
    fi, fj = (fi0, fi1), (fj0, fj1)

    def vid(zz, xx):
        return ((z + zz) % 4) * 4 + (x + xx) % 4

    def uid(yy, cc):
        return ((y + yy) % 4) * 2 + (core + cc) % 2

    own = [pltpu.make_async_copy(vecs, vec, own_sem.at[0])]
    for w in range(WAVES):
        at = fac.at[0, pl.ds(w * ROWS, ROWS)]
        own.append(pltpu.make_async_copy(at, fi[w].at[v], own_sem.at[1 + 2 * w]))
        own.append(pltpu.make_async_copy(at, fj[w].at[u], own_sem.at[2 + 2 * w]))
    greet(u, v)
    for c in own:
        c.start()
    pending = []

    def send(w, from_fac, buf, slot, q, n, sem, dev):
        at = buf[w].at[slot, pl.ds(q, n)]
        src = fac.at[0, pl.ds(w * ROWS + q, n)] if from_fac else at
        c = pltpu.make_async_remote_copy(src, at, sem[0], sem[1], dev, MESH)
        c.start()
        pending.append(c)

    def got(w, buf, slot, q, n, sem, dev):
        at = buf[w].at[slot, pl.ds(q, n)]
        pltpu.make_async_remote_copy(at, at, sem[0], sem[1], dev, MESH).wait_recv()

    def wave(w):
        h = ROWS // 2
        s = h // 2

        def sem(half, k):
            return ss.at[w, half, k], rs.at[w, half, k]

        def csem(k):
            return css.at[w, k], crs.at[w, k]

        halves = []
        for half in (0, 1):
            if half == 0:
                first = lambda d: {"occj": vid(0, d)}
                second = lambda d: {"occj": vid(d, 0)}
                slot = lambda a, b: vid(b, a)
            else:
                first = lambda d: {"occj": vid(d, 0)}
                second = lambda d: {"occj": vid(0, d)}
                slot = lambda a, b: vid(a, b)
            halves.append((half, half * h, first, second, slot))

        def second_send(half, q, second, slot, a, base, mine=False):
            send(w, mine, fi, slot(a, 0), q, h, sem(half, base), second(1))
            send(w, mine, fi, slot(a, 0), q, h, sem(half, base + 1), second(3))

        def second_forward(half, q, second, slot, a, base):
            got(w, fi, slot(a, 3), q, h, sem(half, base), second(1))
            send(w, False, fi, slot(a, 3), q, s, sem(half, base + 2), second(1))
            got(w, fi, slot(a, 1), q, h, sem(half, base + 1), second(1))
            send(w, False, fi, slot(a, 1), q + s, s, sem(half, base + 3), second(3))

        def s0():
            for half, q, first, second, slot in halves:
                send(w, True, fi, v, q, h, sem(half, 0), first(1))
                send(w, True, fi, v, q, h, sem(half, 1), first(3))
            for half, q, first, second, slot in halves:
                second_send(half, q, second, slot, 0, 4, True)
            send(w, True, fj, u, 0, ROWS, csem(0), {"occi": uid(1, 0)})
            send(w, True, fj, u, 0, ROWS, csem(1), {"occi": uid(3, 0)})
            send(w, True, fj, u, 0, ROWS, csem(4), {"occi": uid(0, 1)})

        def s1():
            for half, q, first, second, slot in halves:
                got(w, fi, slot(3, 0), q, h, sem(half, 0), first(1))
                send(w, False, fi, slot(3, 0), q, s, sem(half, 2), first(1))
                got(w, fi, slot(1, 0), q, h, sem(half, 1), first(1))
                send(w, False, fi, slot(1, 0), q + s, s, sem(half, 3), first(3))
            for half, q, first, second, slot in halves:
                second_send(half, q, second, slot, 3, 8)
                second_send(half, q, second, slot, 1, 12)

        def s2():
            for half, q, first, second, slot in halves:
                second_forward(half, q, second, slot, 0, 4)
            n = ROWS // 2
            got(w, fj, uid(3, 0), 0, ROWS, csem(0), {"occi": uid(1, 0)})
            send(w, False, fj, uid(3, 0), 0, n, csem(2), {"occi": uid(1, 0)})
            send(w, False, fj, uid(3, 0), 0, ROWS, csem(5), {"occi": uid(0, 1)})
            got(w, fj, uid(1, 0), 0, ROWS, csem(1), {"occi": uid(1, 0)})
            send(w, False, fj, uid(1, 0), n, n, csem(3), {"occi": uid(3, 0)})
            send(w, False, fj, uid(1, 0), 0, ROWS, csem(6), {"occi": uid(0, 1)})

        def s3():
            for half, q, first, second, slot in halves:
                got(w, fi, slot(2, 0), q, s, sem(half, 2), first(1))
                got(w, fi, slot(2, 0), q + s, s, sem(half, 3), first(1))
                second_send(half, q, second, slot, 2, 16)

        def s4():
            for half, q, first, second, slot in halves:
                second_forward(half, q, second, slot, 3, 8)
                second_forward(half, q, second, slot, 1, 12)
            n = ROWS // 2
            got(w, fj, uid(2, 0), 0, n, csem(2), {"occi": uid(1, 0)})
            got(w, fj, uid(2, 0), n, n, csem(3), {"occi": uid(1, 0)})
            send(w, False, fj, uid(2, 0), 0, ROWS, csem(7), {"occi": uid(0, 1)})

        def s5():
            for half, q, first, second, slot in halves:
                second_forward(half, q, second, slot, 2, 16)

        def s6():
            for half, q, first, second, slot in halves:
                for a, base in ((0, 4), (3, 8), (1, 12), (2, 16)):
                    got(w, fi, slot(a, 2), q, s, sem(half, base + 2), second(1))
                    got(w, fi, slot(a, 2), q + s, s, sem(half, base + 3), second(1))
            for k, yy in ((4, 0), (5, 3), (6, 1), (7, 2)):
                got(w, fj, uid(yy, 1), 0, ROWS, csem(k), {"occi": uid(0, 1)})

        return s0, s1, s2, s3, s4, s5, s6

    def halve(w):
        def bi(k, c):
            h, l = split(fi[w][k])
            th[k] = h
            tl[k] = l
            return c

        def bj(k, c):
            h, l = split(fj[w][k])
            jh[k] = h
            jl[k] = l
            return c

        lax.fori_loop(0, NJ, bi, 0)
        lax.fori_loop(0, NI, bj, 0)

    rows = lax.broadcasted_iota(jnp.int32, (128, 128), 0)
    cols = lax.broadcasted_iota(jnp.int32, (128, 128), 1)

    def pair(w, p):
        oi, oj = occ[0, p], occ[1, p]
        i, j = lax.rem(oi, NJ), lax.div(oj, NJ)
        o = product(th, tl, jh, jl, i, j, vec[p])
        if w == 0:
            acc[p] = o
            return
        den = denominator(en, p) - (eo[oi] + eo[oj])
        n = cnt[p]
        acc[p] = jnp.where((rows < n) & (cols < n), -(acc[p] + o) / den, 0.0)

    def some(w, lo, hi):
        def body(b, c):
            for g in range(GROUP):
                pair(w, b * GROUP + g)
            return c

        lax.fori_loop(lo // GROUP, hi // GROUP, body, 0)

    a, b = wave(0), wave(1)
    a[0]()
    tables(tab, ri, rj, plan, weight)
    waits = []
    for k, off in enumerate(OFF_I + OFF_J):
        if k < 7:
            to, frm, me, r, q, name = peer_i(u, off), peer_i(u, back(off, (4, 2))), u, ri, qi, "occi"
        else:
            to, frm, me, r, q, name = peer_j(v, off), peer_j(v, back(off, (4, 4))), v, rj, qj, "occj"
        c = pltpu.make_async_remote_copy(r.at[to], q.at[me], tab_sem.at[0, k], tab_sem.at[1, k], {name: to}, MESH)
        c.start()
        pending.append(c)
        waits.append(
            pltpu.make_async_remote_copy(r.at[frm], q.at[frm], tab_sem.at[0, k], tab_sem.at[1, k], {name: to}, MESH)
        )
    qi[u] = ri[u]
    qj[v] = rj[v]
    for step in (a[1], b[0], a[2], a[3], b[1], a[4], b[2], a[5], b[3]):
        step()
    for c in own:
        c.wait()
    a[6]()
    halve(0)
    some(0, 0, 16)
    b[4]()
    some(0, 16, 32)
    b[5]()
    some(0, 32, 64)
    b[6]()
    halve(1)
    outs = []
    for k in range(4):
        some(1, 16 * k, 16 * k + 16)
        part = pl.ds(16 * k, 16)
        c = pltpu.make_async_copy(acc.at[part], amp.at[part], out_sem.at[k])
        c.start()
        outs.append(c)
    for c in waits:
        c.wait_recv()
    for c in pending:
        c.wait_send()
    for c in outs:
        c.wait()


def dot_0(a, b):
    return lax.dot_general(a, b, (((0,), (0,)), ((), ())), preferred_element_type=f32)


def product(th, tl, jh, jl, i, j, vec):
    vth, vtl = split(jnp.transpose(vec))
    v2 = jnp.concatenate([vth, vtl], axis=0)
    a = dot_t(v2, th[i])
    lt = a[:128] + a[128:] + dot_t(vth, tl[i])
    b = dot_t(v2, jh[j])
    rt = b[:128] + b[128:] + dot_t(vth, jl[j])
    lh, ll = split(lt)
    rh, rl = split(rt)
    o = dot_t(jnp.concatenate([lh, ll], axis=0), jnp.concatenate([rh, rl], axis=0))
    return (o[:128, :128] + o[:128, 128:]) + o[128:, :128]


def denominator(en, p):
    across = jnp.broadcast_to(en[pl.ds(p, 1), :], (128, 128))
    return jnp.transpose(across) + across


def integrals(occ, cnt, eo, tab, en, factors, vecs):
    smem = pl.BlockSpec(memory_space=pltpu.SMEM)
    vmem = pl.BlockSpec(memory_space=pltpu.VMEM)
    anyw = pl.BlockSpec(memory_space=pl.ANY)
    i32 = jnp.int32
    dma = pltpu.SemaphoreType.DMA
    return pl.pallas_call(
        integral_kernel,
        out_shape=(
            jax.ShapeDtypeStruct((NP, 128, 128), f32),
            jax.ShapeDtypeStruct((NI, 1, 128), i32),
            jax.ShapeDtypeStruct((NJ, 1, 128), i32),
            jax.ShapeDtypeStruct((8, 128), i32),
            jax.ShapeDtypeStruct((1, 128), f32),
        ),
        in_specs=[smem] * 3 + [vmem] * 2 + [anyw] * 2,
        out_specs=(anyw, vmem, vmem, vmem, vmem),
        scratch_shapes=[
            pltpu.VMEM((NJ, ROWS, 256), f32),
            pltpu.VMEM((NJ, ROWS, 256), f32),
            pltpu.VMEM((NI, ROWS, 256), f32),
            pltpu.VMEM((NI, ROWS, 256), f32),
            pltpu.VMEM((NJ, ROWS, 256), bf16),
            pltpu.VMEM((NJ, ROWS, 256), bf16),
            pltpu.VMEM((NI, ROWS, 256), bf16),
            pltpu.VMEM((NI, ROWS, 256), bf16),
            pltpu.VMEM((NP, 256, 128), f32),
            pltpu.VMEM((NP, 128, 128), f32),
            pltpu.VMEM((NI, 1, 128), i32),
            pltpu.VMEM((NJ, 1, 128), i32),
            dma((5,)),
            dma((2, 22)),
            dma((WAVES, 2, 20)),
            dma((WAVES, 2, 20)),
            dma((WAVES, 8)),
            dma((WAVES, 8)),
            dma((4,)),
        ],
        compiler_params=pltpu.CompilerParams(collective_id=0, has_side_effects=True, vmem_limit_bytes=VMEM_ALL),
    )(occ, cnt, eo, tab, en, factors, vecs)


UNROLL = 4
SLOTS = NI * CAPI + NJ * CAPJ


def couple(plan, weight, corr, arrived, term):
    term[NC] = jnp.zeros((128, 128), f32)

    def body(b, run):
        for k in range(UNROLL):
            s = b * UNROLL + k
            m = corr[plan[0, s]]
            mh, ml = split(m)
            xh, xl = split(arrived[plan[1, s]])
            xx = jnp.concatenate([xh, xl], axis=1)
            h = dot(jnp.concatenate([mh, ml], axis=1), jnp.concatenate([xx, xx], axis=0))
            hh, hl = split(h[:, :128] + h[:, 128:])
            m4 = jnp.concatenate([jnp.concatenate([mh, mh], axis=1), jnp.concatenate([ml, ml], axis=1)], axis=0)
            t = dot_t(jnp.concatenate([hh, hl], axis=1), m4)
            t = (t[:, :128] + t[:, 128:]) * weight[0, s]
            run = jnp.where(plan[2, s] > 0, run, 0.0) + t
            term[s] = run
        return run

    lax.fori_loop(0, NC // UNROLL, body, jnp.zeros((128, 128), f32))


def iterate_kernel(
    qi, qj, plan, weight, occ, cnt, eo, en, amp0, ci, cj, amp_out, res_out,
    amp, inv, corr, delta, term, snd_i, snd_j, mid, rcv0, rcv1, ls, si, ri, sj, rj,
):
    u = lax.axis_index("occi")
    v = lax.axis_index("occj")
    x, z = v % 4, v // 4
    rows = lax.broadcasted_iota(jnp.int32, (128, 128), 0)
    cols = lax.broadcasted_iota(jnp.int32, (128, 128), 1)
    loads = [
        pltpu.make_async_copy(amp0, amp, ls.at[0]),
        pltpu.make_async_copy(ci, corr.at[pl.ds(0, 32)], ls.at[1]),
        pltpu.make_async_copy(cj, corr.at[pl.ds(32, 32)], ls.at[2]),
    ]
    for c in loads:
        c.start()
    greet(u, v)

    def vid(dz, dx):
        return ((z + dz) % 4) * 4 + (x + dx) % 4

    def exchange(it, src, arrived, beside):
        half_rows = CAPJ // 2
        first, rest, sent = {}, [], []

        def fill(half, d):
            for e in range(4):
                if d == 0 and e == 0:
                    continue
                to = vid(e, d) if half == 0 else vid(d, e)
                for s in range(half_rows):
                    snd_j[it, half, d, half_rows * e + s] = src[qj[to, 0, half_rows * half + s]]

        def place(half, d, e):
            frm = vid((4 - e) % 4, (4 - d) % 4) if half == 0 else vid((4 - d) % 4, (4 - e) % 4)
            return arrived.at[pl.ds(NI * CAPI + frm * CAPJ + half_rows * half, half_rows)]

        for d in (2, 1, 3):
            for half in (0, 1):
                fill(half, d)
                to = vid(0, d) if half == 0 else vid(d, 0)
                c = pltpu.make_async_remote_copy(
                    snd_j.at[it, half, d], mid.at[it, half, d], sj.at[it, half, d, 0], rj.at[it, half, d, 0], {"occj": to}, MESH
                )
                c.start()
                first[half, d] = c
                sent.append(c)
        for k, off in enumerate(OFF_I):
            to, frm = peer_i(u, off), peer_i(u, back(off, (4, 2)))
            for s in range(CAPI):
                snd_i[it, k * CAPI + s] = src[qi[to, 0, s]]
            out = snd_i.at[it, pl.ds(k * CAPI, CAPI)]
            c = pltpu.make_async_remote_copy(
                out, arrived.at[pl.ds(u * CAPI, CAPI)], si.at[it, k], ri.at[it, k], {"occi": to}, MESH
            )
            c.start()
            sent.append(c)
            rest.append(
                pltpu.make_async_remote_copy(
                    out, arrived.at[pl.ds(frm * CAPI, CAPI)], si.at[it, k], ri.at[it, k], {"occi": to}, MESH
                )
            )

        def onward(half, d):
            for e in (2, 1, 3):
                to = vid(e, 0) if half == 0 else vid(0, e)
                out = (snd_j if d == 0 else mid).at[it, half, d, pl.ds(half_rows * e, half_rows)]
                start = vid(0, (4 - d) % 4) if half == 0 else vid((4 - d) % 4, 0)
                into = arrived.at[pl.ds(NI * CAPI + start * CAPJ + half_rows * half, half_rows)]
                c = pltpu.make_async_remote_copy(
                    out, into, sj.at[it, half, d, e], rj.at[it, half, d, e], {"occj": to}, MESH
                )
                c.start()
                sent.append(c)
                rest.append(
                    pltpu.make_async_remote_copy(
                        out, place(half, d, e), sj.at[it, half, d, e], rj.at[it, half, d, e], {"occj": to}, MESH
                    )
                )

        for half in (0, 1):
            fill(half, 0)
            onward(half, 0)
        for s in range(CAPI):
            arrived[u * CAPI + s] = src[qi[u, 0, s]]
        for s in range(CAPJ):
            arrived[NI * CAPI + v * CAPJ + s] = src[qj[v, 0, s]]
        beside(0)
        for d in (1, 3, 2):
            for half in (0, 1):
                first[half, d].wait_recv()
                onward(half, d)
            if d == 3:
                beside(1)
        for half in (0, 1):
            for d in (1, 3, 2):
                frm = vid(0, (4 - d) % 4) if half == 0 else vid((4 - d) % 4, 0)
                for s in range(half_rows):
                    arrived[NI * CAPI + frm * CAPJ + half_rows * half + s] = mid[it, half, d, s]
        beside(2)
        for c in rest:
            c.wait_recv()
        for c in sent:
            c.wait_send()

    def inverses(lo, hi):
        def body(p, carry):
            den = denominator(en, p) - (eo[occ[0, p]] + eo[occ[1, p]])
            n = cnt[p]
            inv[p] = jnp.where((rows < n) & (cols < n), 1.0 / den, 0.0)
            return carry

        lax.fori_loop(lo, hi, body, 0)

    def beside0(part):
        if part == 0:
            inverses(0, 16)
        elif part == 1:
            inverses(16, 32)
        else:
            inverses(32, 64)
            for c in loads[1:]:
                c.wait()

    loads[0].wait()
    exchange(0, amp, rcv0, beside0)
    couple(plan, weight, corr, rcv0, term)

    def first(p, carry):
        delta[p] = term[plan[3, p]] * inv[p]
        return carry

    lax.fori_loop(0, NP, first, 0)

    def beside1(part):
        if part == 1:

            def add(p, carry):
                amp[p] = amp[p] + delta[p]
                return carry

            lax.fori_loop(0, NP, add, 0)

    exchange(1, delta, rcv1, beside1)
    couple(plan, weight, corr, rcv1, term)

    def second(p, carry):
        s = term[plan[3, p]]
        n = cnt[p]
        amp[p] = amp[p] + s * inv[p]
        inv[p] = jnp.where((rows < n) & (cols < n), -s, 0.0)
        return carry

    lax.fori_loop(0, NP, second, 0)
    outs = [pltpu.make_async_copy(amp, amp_out, ls.at[0]), pltpu.make_async_copy(inv, res_out, ls.at[1])]
    for c in outs:
        c.start()
    for c in outs:
        c.wait()


def iterate(qi, qj, plan, weight, occ, cnt, eo, en, amp, ci, cj):
    smem = pl.BlockSpec(memory_space=pltpu.SMEM)
    vmem = pl.BlockSpec(memory_space=pltpu.VMEM)
    anyw = pl.BlockSpec(memory_space=pl.ANY)
    dma = pltpu.SemaphoreType.DMA
    mats = lambda *n: pltpu.VMEM(n + (128, 128), f32)
    return pl.pallas_call(
        iterate_kernel,
        out_shape=(jax.ShapeDtypeStruct((NP, 128, 128), f32),) * 2,
        in_specs=[smem] * 7 + [vmem] + [anyw] * 3,
        out_specs=(anyw, anyw),
        scratch_shapes=[
            mats(NP),
            mats(NP),
            mats(NC),
            mats(NP),
            mats(NC + 1),
            mats(2, 7 * CAPI),
            mats(2, 2, 4, 2 * CAPJ),
            mats(2, 2, 4, 2 * CAPJ),
            mats(SLOTS),
            mats(SLOTS),
            dma((3,)),
            dma((2, 7)),
            dma((2, 7)),
            dma((2, 2, 4, 4)),
            dma((2, 2, 4, 4)),
        ],
        compiler_params=pltpu.CompilerParams(collective_id=1, has_side_effects=True, vmem_limit_bytes=VMEM_ALL),
    )(qi, qj, plan, weight, occ, cnt, eo, en, amp, ci, cj)


def row(i_list, j_list, fill):
    rest = jnp.full((128 - 64,), fill, f32)
    return jnp.concatenate([i_list.astype(f32), j_list.astype(f32), rest])


def local(
    factors, pno_vecs, pair_occ, pno_count, pno_energy, occ_energy,
    coupi_peer, coupi_slot, coupi_target, coupi_fock, coupi_correlation,
    coupj_peer, coupj_slot, coupj_target, coupj_fock, coupj_correlation,
):
    none = jnp.zeros((128,), f32)
    tab = jnp.stack(
        [
            row(coupi_peer[:, 0], coupj_peer[:, 0] + NI, -1.0),
            row(coupi_slot, coupj_slot, 0.0),
            row(coupi_target, coupj_target, 1000.0),
            row(coupi_fock, coupj_fock, 0.0),
            none, none, none, none,
        ]
    )
    occ = pair_occ.T
    amp, qi, qj, plan, weight = integrals(occ, pno_count, occ_energy, tab, pno_energy, factors, pno_vecs)
    return iterate(
        qi, qj, plan, weight, occ, pno_count, occ_energy, pno_energy, amp, coupi_correlation, coupj_correlation
    )


def solution(mesh):
    both = ("occi", "occj")
    three, two, one = P(both, None, None), P(both, None), P(both)
    placed = (
        three, three, two, one, two, P(),
        two, one, one, one, three,
        two, one, one, one, three,
    )
    return jax.shard_map(local, mesh=mesh, in_specs=placed, out_specs=(three, three), check_vma=False)
```

time: 680 us -> 236 us (0.35)
  waiting for transfers between devices: 254 us -> 0 us
  Pallas kernels: 0 us -> 224 us
  matrix products: 192 us -> 0 us
  local copies, waits for them, and re-layouts: 171 us -> 7.48 us
  starting transfers between devices: 35.2 us -> 0 us
  between operations: 14.7 us -> 0.66 us
    pallas_call x0 -> x2, Pallas kernels: none -> 224 us  [the longest x1 125 us: iterate(): pl.pallas_call(iterate_kernel, out_shape=(jax.ShapeDtypeStruct((NP, 128,...]
    dot_general x36 -> x0, matrix products: 192 us -> none  [the longest x8 66.1 us: integrals(): jnp.einsum('gqv,gva->gqa', left_factor, vectors, precision=highest)]
    all_to_all x6 -> x0, waiting for transfers between devices: 177 us -> none  [the longest x2 88.8 us: local(): lax.all_to_all(select_rows(amplitude, incoming_j), 'occj', split_axis=0,...]
    gather x34 -> x0, local copies, waits for them, and re-layouts: 141 us -> none  [the longest x8 49.7 us: integrals(): left_factor = block_first[rows_first]]
    all_gather x2 -> x0, waiting for transfers between devices: 75.9 us -> none  [the longest x1 72.6 us: local(): block_first = lax.all_gather(factors, 'occj', axis=0, tiled=True)]
    all_to_all x6 -> x0, starting transfers between devices: 35.1 us -> none  [the longest x2 11.6 us: local(): lax.all_to_all(select_rows(amplitude, incoming_i), 'occi', split_axis=0,...]
    dynamic_update_slice x8 -> x0, local copies, waits for them, and re-layouts: 8.85 us -> none  [local(): lax.map(integrals, (local_first[padded_rows].reshape(group_count, 8), loc...]
  transfers between devices with their start and end apart: 8 -> 0, of which waited for: 6 -> 0; matrix products, arithmetic and copies ran while one was open for 46% -> 0% of each run, Pallas kernels for 0% -> 0%
where the time goes in v2:
time: 236 us
  Pallas kernels  224 us (95%)
  local copies, waits for them, and re-layouts  7.48 us (3%)
  other arithmetic  4.13 us (2%)
    pallas_call x1, Pallas kernels, iterate(): pl.pallas_call(iterate_kernel, out_shape=(jax.ShapeDtypeStruct((NP, 128,...  125 us
    pallas_call x1, Pallas kernels, integrals(): pl.pallas_call(integral_kernel, out_shape=(jax.ShapeDtypeStruct((NP, 128,...  98.9 us
    unnamed x4, local copies, waits for them, and re-layouts  6.87 us

profile of v2, /device:TPU:1, one launch (start us, length us, event | category | flops | bytes accessed | tf_op | source)
XLA Modules:
  0.0 235.9 jit_solution(493462849256260698)
XLA Ops:
  0.6 0.7 convert_element_type.28
  1.3 0.7 convert_element_type.30
  1.9 0.7 convert_element_type.29
  2.6 0.7 convert_element_type.31
  3.3 0.7 fusion.1
  4.0 0.7 convert_bitcast_fusion
  4.7 0.1 maximum_bitcast_fusion
  4.8 0.6 stack.23.tab
  5.4 98.9 %shard_map.167 = (f32[64,128,128]{2,1,0:T(8,128)}, s32[8,1,128]{2,1,0:T(1,128)}, s32[16,1,128]{2,1,0:T(1,128)}, s32[8,128]{1,0:T(8,128)}, f32[1,128]{1,0:T(1,128)}) custom-call(s32[2,64]{1,0:T(2,128)} %bitcast.13, s32[64]{0:T(128)} %cnt.3, f32[128]{0:T(128)} %eo.3, f32[8,128]{1,0:T(8,128)} %stack.23.tab, f32[64,128]{1,0:T(8,128)} %en.3, f32[1,512,256]{2,1,0:T(8,128)} %fac.1, ...), custom_call_target="tpu_custom_call" | custom-call | tf_op jit(solution)/shard_map/pallas_call | solution.py:341
  104.3 124.7 %shard_map.168 = (f32[64,128,128]{2,1,0:T(8,128)}, f32[64,128,128]{2,1,0:T(8,128)}) custom-call(s32[8,1,128]{2,1,0:T(1,128)} %get-tuple-element.7.qi, s32[16,1,128]{2,1,0:T(1,128)} %get-tuple-element.8.qj, s32[8,128]{1,0:T(8,128)} %get-tuple-element.9.plan, f32[1,128]{1,0:T(1,128)} %get-tuple-element.10.weight, s32[2,64]{1,0:T(2,128)} %bitcast.14, s32[64]{0:T(128)} %cnt.3, ...), custom_call_target="tpu_custom_call" | custom-call | tf_op jit(solution)/shard_map/pallas_call | solution.py:570
  229.0 0.0 copy-start
  229.0 4.8 %copy.20 = f32[64,128,128]{2,1,0:T(8,128)} copy(f32[64,128,128]{2,1,0:T(8,128)} %get-tuple-element.19) | data formatting | bytes 8388608
  233.9 0.0 copy-done
  233.9 2.0 copy.21
  (4 shorter events, 0.0 us)
Async XLA Ops:
  229.0 4.9 %copy-start = (f32[64,128,128]{2,1,0:T(8,128)S(1)}, f32[64,128,128]{2,1,0:T(8,128)}, u32[]{:S(2)}) copy-start(f32[64,128,128]{2,1,0:T(8,128)} %get-tuple-element.20) | copy-start | bytes 12582916

commit v3 on v2

--- a/solution.py
+++ b/solution.py
@@ -17,7 +17,7 @@
 WAVES = 2
 ROWS = 512 // WAVES
 VMEM_ALL = 60 * 2**20
-GROUP = 4
+GROUP = 8
 
 OFF_I = [(2, 0), (2, 1), (1, 0), (3, 0), (1, 1), (3, 1), (0, 1)]
 OFF_J = sorted(
@@ -100,13 +100,14 @@
 
 def integral_kernel(
     occ, cnt, eo, tab, en, fac, vecs, amp, qi, qj, plan, weight,
-    fi0, fi1, fj0, fj1, th, tl, jh, jl, vec, acc, ri, rj, own_sem, tab_sem, rs, ss, crs, css, out_sem,
+    fi0, fi1, fj0, fj1, th0, th1, tl0, tl1, jh0, jh1, jl0, jl1, vec, both, acc, ri, rj, own_sem, tab_sem, rs, ss, crs, css, out_sem,
 ):
     u = lax.axis_index("occi")
     v = lax.axis_index("occj")
     x, z = v % 4, v // 4
     y, core = u // 2, u % 2
     fi, fj = (fi0, fi1), (fj0, fj1)
+    th, tl, jh, jl = (th0, th1), (tl0, tl1), (jh0, jh1), (jl0, jl1)
 
     def vid(zz, xx):
         return ((z + zz) % 4) * 4 + (x + xx) % 4
@@ -227,44 +228,64 @@
 
         return s0, s1, s2, s3, s4, s5, s6
 
-    def halve(w):
-        def bi(k, c):
-            h, l = split(fi[w][k])
-            th[k] = h
-            tl[k] = l
+    def halve_i(w, blocks):
+        for dz, dx in blocks:
+            k = vid(dz, dx)
+            th[w][k], tl[w][k] = split(fi[w][k])
+
+    def halve_j(w):
+        def body(k, c):
+            jh[w][k], jl[w][k] = split(fj[w][k])
             return c
 
-        def bj(k, c):
-            h, l = split(fj[w][k])
-            jh[k] = h
-            jl[k] = l
+        lax.fori_loop(0, NI, body, 0)
+
+    def halve_vectors():
+        def body(b, c):
+            for k in range(2):
+                h, l = split(vec[2 * b + k])
+                both[2 * b + k] = jnp.concatenate([h, l], axis=1)
             return c
 
-        lax.fori_loop(0, NJ, bi, 0)
-        lax.fori_loop(0, NI, bj, 0)
+        lax.fori_loop(0, NP // 2, body, 0)
 
     rows = lax.broadcasted_iota(jnp.int32, (128, 128), 0)
     cols = lax.broadcasted_iota(jnp.int32, (128, 128), 1)
 
-    def pair(w, p):
-        oi, oj = occ[0, p], occ[1, p]
-        i, j = lax.rem(oi, NJ), lax.div(oj, NJ)
-        o = product(th, tl, jh, jl, i, j, vec[p])
-        if w == 0:
-            acc[p] = o
-            return
-        den = denominator(en, p) - (eo[oi] + eo[oj])
-        n = cnt[p]
-        acc[p] = jnp.where((rows < n) & (cols < n), -(acc[p] + o) / den, 0.0)
-
     def some(w, lo, hi):
         def body(b, c):
-            for g in range(GROUP):
-                pair(w, b * GROUP + g)
+            group = [b * GROUP + g for g in range(GROUP)]
+            stage = []
+            for p in group:
+                i, j = lax.rem(occ[0, p], NJ), lax.div(occ[1, p], NJ)
+                hl = both[p]
+                h = hl[:, :128]
+                one = dot(th[w][i], hl)
+                left = one[:, :128] + one[:, 128:] + dot(tl[w][i], h)
+                two = dot(jh[w][j], hl)
+                right = two[:, :128] + two[:, 128:] + dot(jl[w][j], h)
+                stage.append((left, right))
+            stage = [
+                (jnp.concatenate(split(left), axis=1), jnp.concatenate(split(right), axis=1)) for left, right in stage
+            ]
+            stage = [dot_0(left, right) for left, right in stage]
+            stage = [(o[:128, :128] + o[:128, 128:]) + o[128:, :128] for o in stage]
+            if w == 0:
+                for p, o in zip(group, stage):
+                    acc[p] = o
+                return c
+            sums = [denominator(en, p) for p in group]
+            for p, o, den in zip(group, stage, sums):
+                den = den - (eo[occ[0, p]] + eo[occ[1, p]])
+                n = cnt[p]
+                acc[p] = jnp.where((rows < n) & (cols < n), -(acc[p] + o) / den, 0.0)
             return c
 
         lax.fori_loop(lo // GROUP, hi // GROUP, body, 0)
 
+    near = [(0, 0), (0, 1), (0, 3), (1, 0), (3, 0)]
+    middle = [(1, 1), (1, 3), (3, 1), (3, 3)]
+    far = [(0, 2), (2, 0), (1, 2), (3, 2), (2, 1), (2, 3), (2, 2)]
     a, b = wave(0), wave(1)
     a[0]()
     tables(tab, ri, rj, plan, weight)
@@ -282,19 +303,34 @@
         )
     qi[u] = ri[u]
     qj[v] = rj[v]
-    for step in (a[1], b[0], a[2], a[3], b[1], a[4], b[2], a[5], b[3]):
-        step()
-    for c in own:
+    a[1]()
+    b[0]()
+    own[0].wait()
+    halve_vectors()
+    a[2]()
+    a[3]()
+    b[1]()
+    for c in own[1:]:
         c.wait()
+    halve_i(0, near)
+    a[4]()
+    b[2]()
+    halve_i(1, near)
+    a[5]()
+    b[3]()
+    halve_i(0, middle)
     a[6]()
-    halve(0)
+    halve_i(0, far)
+    halve_j(0)
     some(0, 0, 16)
     b[4]()
     some(0, 16, 32)
     b[5]()
+    halve_i(1, middle)
     some(0, 32, 64)
     b[6]()
-    halve(1)
+    halve_i(1, far)
+    halve_j(1)
     outs = []
     for k in range(4):
         some(1, 16 * k, 16 * k + 16)
@@ -312,19 +348,6 @@
 
 def dot_0(a, b):
     return lax.dot_general(a, b, (((0,), (0,)), ((), ())), preferred_element_type=f32)
-
-
-def product(th, tl, jh, jl, i, j, vec):
-    vth, vtl = split(jnp.transpose(vec))
-    v2 = jnp.concatenate([vth, vtl], axis=0)
-    a = dot_t(v2, th[i])
-    lt = a[:128] + a[128:] + dot_t(vth, tl[i])
-    b = dot_t(v2, jh[j])
-    rt = b[:128] + b[128:] + dot_t(vth, jl[j])
-    lh, ll = split(lt)
-    rh, rl = split(rt)
-    o = dot_t(jnp.concatenate([lh, ll], axis=0), jnp.concatenate([rh, rl], axis=0))
-    return (o[:128, :128] + o[:128, 128:]) + o[128:, :128]
 
 
 def denominator(en, p):
@@ -354,11 +377,10 @@
             pltpu.VMEM((NJ, ROWS, 256), f32),
             pltpu.VMEM((NI, ROWS, 256), f32),
             pltpu.VMEM((NI, ROWS, 256), f32),
-            pltpu.VMEM((NJ, ROWS, 256), bf16),
-            pltpu.VMEM((NJ, ROWS, 256), bf16),
-            pltpu.VMEM((NI, ROWS, 256), bf16),
-            pltpu.VMEM((NI, ROWS, 256), bf16),
+            *[pltpu.VMEM((NJ, ROWS, 256), bf16)] * 4,
+            *[pltpu.VMEM((NI, ROWS, 256), bf16)] * 4,
             pltpu.VMEM((NP, 256, 128), f32),
+            pltpu.VMEM((NP, 256, 256), bf16),
             pltpu.VMEM((NP, 128, 128), f32),
             pltpu.VMEM((NI, 1, 128), i32),
             pltpu.VMEM((NJ, 1, 128), i32),
@@ -374,7 +396,7 @@
     )(occ, cnt, eo, tab, en, factors, vecs)
 
 
-UNROLL = 4
+UNROLL = 8
 SLOTS = NI * CAPI + NJ * CAPJ
 
 
@@ -382,16 +404,21 @@
     term[NC] = jnp.zeros((128, 128), f32)
 
     def body(b, run):
-        for k in range(UNROLL):
-            s = b * UNROLL + k
-            m = corr[plan[0, s]]
-            mh, ml = split(m)
+        places = [b * UNROLL + k for k in range(UNROLL)]
+        corrs = [split(corr[plan[0, s]]) for s in places]
+        stage = []
+        for s, (mh, ml) in zip(places, corrs):
             xh, xl = split(arrived[plan[1, s]])
             xx = jnp.concatenate([xh, xl], axis=1)
-            h = dot(jnp.concatenate([mh, ml], axis=1), jnp.concatenate([xx, xx], axis=0))
-            hh, hl = split(h[:, :128] + h[:, 128:])
-            m4 = jnp.concatenate([jnp.concatenate([mh, mh], axis=1), jnp.concatenate([ml, ml], axis=1)], axis=0)
-            t = dot_t(jnp.concatenate([hh, hl], axis=1), m4)
+            stage.append((jnp.concatenate([mh, ml], axis=1), jnp.concatenate([xx, xx], axis=0)))
+        stage = [dot(m, x) for m, x in stage]
+        stage = [jnp.concatenate(split(h[:, :128] + h[:, 128:]), axis=1) for h in stage]
+        corrs = [
+            jnp.concatenate([jnp.concatenate([mh, mh], axis=1), jnp.concatenate([ml, ml], axis=1)], axis=0)
+            for mh, ml in corrs
+        ]
+        stage = [dot_t(h, m) for h, m in zip(stage, corrs)]
+        for s, t in zip(places, stage):
             t = (t[:, :128] + t[:, 128:]) * weight[0, s]
             run = jnp.where(plan[2, s] > 0, run, 0.0) + t
             term[s] = run
@@ -528,11 +555,13 @@
     exchange(0, amp, rcv0, beside0)
     couple(plan, weight, corr, rcv0, term)
 
-    def first(p, carry):
-        delta[p] = term[plan[3, p]] * inv[p]
+    def first(b, carry):
+        for k in range(4):
+            p = 4 * b + k
+            delta[p] = term[plan[3, p]] * inv[p]
         return carry
 
-    lax.fori_loop(0, NP, first, 0)
+    lax.fori_loop(0, NP // 4, first, 0)
 
     def beside1(part):
         if part == 1:
@@ -546,14 +575,16 @@
     exchange(1, delta, rcv1, beside1)
     couple(plan, weight, corr, rcv1, term)
 
-    def second(p, carry):
-        s = term[plan[3, p]]
-        n = cnt[p]
-        amp[p] = amp[p] + s * inv[p]
-        inv[p] = jnp.where((rows < n) & (cols < n), -s, 0.0)
+    def second(b, carry):
+        for k in range(4):
+            p = 4 * b + k
+            s = term[plan[3, p]]
+            n = cnt[p]
+            amp[p] = amp[p] + s * inv[p]
+            inv[p] = jnp.where((rows < n) & (cols < n), -s, 0.0)
         return carry
 
-    lax.fori_loop(0, NP, second, 0)
+    lax.fori_loop(0, NP // 4, second, 0)
     outs = [pltpu.make_async_copy(amp, amp_out, ls.at[0]), pltpu.make_async_copy(inv, res_out, ls.at[1])]
     for c in outs:
         c.start()

time: 236 us -> 206 us (0.87)
  Pallas kernels: 224 us -> 193 us
    pallas_call x1, Pallas kernels: 98.9 us -> 74.6 us  [integrals(): pl.pallas_call(integral_kernel, out_shape=(jax.ShapeDtypeStruct((NP, 128,...]
    pallas_call x1, Pallas kernels: 125 us -> 119 us  [iterate(): pl.pallas_call(iterate_kernel, out_shape=(jax.ShapeDtypeStruct((NP, 128,...]
where the time goes in v3:
time: 206 us; the launch traced here: 205 us
  Pallas kernels  193 us (94%)
  local copies, waits for them, and re-layouts  7.48 us (4%)
  other arithmetic  4.13 us (2%)
    pallas_call x1, Pallas kernels, iterate(): pl.pallas_call(iterate_kernel, out_shape=(jax.ShapeDtypeStruct((NP, 128,...  119 us
    pallas_call x1, Pallas kernels, integrals(): pl.pallas_call(integral_kernel, out_shape=(jax.ShapeDtypeStruct((NP, 128,...  74.6 us
    unnamed x4, local copies, waits for them, and re-layouts  6.87 us

profile of v3, /device:TPU:1, one launch (start us, length us, event | category | flops | bytes accessed | tf_op | source)
XLA Modules:
  0.0 205.4 jit_solution(3366170219826887503)
XLA Ops:
  0.6 0.7 convert_element_type.28
  1.3 0.7 convert_element_type.30
  1.9 0.7 convert_element_type.29
  2.6 0.7 convert_element_type.31
  3.3 0.7 fusion.1
  4.0 0.7 convert_bitcast_fusion
  4.7 0.1 maximum_bitcast_fusion
  4.8 0.6 stack.23.tab
  5.4 74.6 %shard_map.167 = (f32[64,128,128]{2,1,0:T(8,128)}, s32[8,1,128]{2,1,0:T(1,128)}, s32[16,1,128]{2,1,0:T(1,128)}, s32[8,128]{1,0:T(8,128)}, f32[1,128]{1,0:T(1,128)}) custom-call(s32[2,64]{1,0:T(2,128)} %bitcast.13, s32[64]{0:T(128)} %cnt.3, f32[128]{0:T(128)} %eo.3, f32[8,128]{1,0:T(8,128)} %stack.23.tab, f32[64,128]{1,0:T(8,128)} %en.3, f32[1,512,256]{2,1,0:T(8,128)} %fac.1, ...), custom_call_target="tpu_custom_call" | custom-call | tf_op jit(solution)/shard_map/pallas_call | solution.py:364
  80.0 118.5 %shard_map.168 = (f32[64,128,128]{2,1,0:T(8,128)}, f32[64,128,128]{2,1,0:T(8,128)}) custom-call(s32[8,1,128]{2,1,0:T(1,128)} %get-tuple-element.7.qi, s32[16,1,128]{2,1,0:T(1,128)} %get-tuple-element.8.qj, s32[8,128]{1,0:T(8,128)} %get-tuple-element.9.plan, f32[1,128]{1,0:T(1,128)} %get-tuple-element.10.weight, s32[2,64]{1,0:T(2,128)} %bitcast.14, s32[64]{0:T(128)} %cnt.3, ...), custom_call_target="tpu_custom_call" | custom-call | tf_op jit(solution)/shard_map/pallas_call | solution.py:601
  198.5 0.0 copy-start
  198.5 4.8 %copy.20 = f32[64,128,128]{2,1,0:T(8,128)} copy(f32[64,128,128]{2,1,0:T(8,128)} %get-tuple-element.19) | data formatting | bytes 8388608
  203.4 0.0 copy-done
  203.4 2.0 copy.21
  (4 shorter events, 0.0 us)
Async XLA Ops:
  198.5 4.9 %copy-start = (f32[64,128,128]{2,1,0:T(8,128)S(1)}, f32[64,128,128]{2,1,0:T(8,128)}, u32[]{:S(2)}) copy-start(f32[64,128,128]{2,1,0:T(8,128)} %get-tuple-element.20) | copy-start | bytes 12582916

commit v4 on v3

--- a/solution.py
+++ b/solution.py
@@ -99,8 +99,8 @@
 
 
 def integral_kernel(
-    occ, cnt, eo, tab, en, fac, vecs, amp, qi, qj, plan, weight,
-    fi0, fi1, fj0, fj1, th0, th1, tl0, tl1, jh0, jh1, jl0, jl1, vec, both, acc, ri, rj, own_sem, tab_sem, rs, ss, crs, css, out_sem,
+    occ, cnt, eo, pi, pj, si, sj, ti, tj, ki, kj, en, fac, vecs, amp, qi, qj, plan, weight,
+    fi0, fi1, fj0, fj1, th0, th1, tl0, tl1, jh0, jh1, jl0, jl1, vec, both, acc, tab, ri, rj, own_sem, tab_sem, rs, ss, crs, css, out_sem,
 ):
     u = lax.axis_index("occi")
     v = lax.axis_index("occj")
@@ -288,7 +288,12 @@
     far = [(0, 2), (2, 0), (1, 2), (3, 2), (2, 1), (2, 3), (2, 2)]
     a, b = wave(0), wave(1)
     a[0]()
+    for r, (one, two, fill) in enumerate(((pi, pj, -1.0), (si, sj, 0.0), (ti, tj, 1000.0), (ki, kj, 0.0))):
+        tab[pl.ds(r, 1), :] = jnp.full((1, 128), fill, f32)
+        tab[pl.ds(r, 1), 0:32] = one[...].astype(f32)
+        tab[pl.ds(r, 1), 32:64] = two[...].astype(f32) + (float(NI) if r == 0 else 0.0)
     tables(tab, ri, rj, plan, weight)
+    b[0]()
     waits = []
     for k, off in enumerate(OFF_I + OFF_J):
         if k < 7:
@@ -304,21 +309,20 @@
     qi[u] = ri[u]
     qj[v] = rj[v]
     a[1]()
-    b[0]()
+    a[2]()
+    a[3]()
     own[0].wait()
     halve_vectors()
-    a[2]()
-    a[3]()
     b[1]()
     for c in own[1:]:
         c.wait()
     halve_i(0, near)
     a[4]()
+    halve_i(0, middle)
+    a[5]()
     b[2]()
     halve_i(1, near)
-    a[5]()
     b[3]()
-    halve_i(0, middle)
     a[6]()
     halve_i(0, far)
     halve_j(0)
@@ -326,8 +330,8 @@
     b[4]()
     some(0, 16, 32)
     b[5]()
+    some(0, 32, 64)
     halve_i(1, middle)
-    some(0, 32, 64)
     b[6]()
     halve_i(1, far)
     halve_j(1)
@@ -355,7 +359,7 @@
     return jnp.transpose(across) + across
 
 
-def integrals(occ, cnt, eo, tab, en, factors, vecs):
+def integrals(occ, cnt, eo, lists, en, factors, vecs):
     smem = pl.BlockSpec(memory_space=pltpu.SMEM)
     vmem = pl.BlockSpec(memory_space=pltpu.VMEM)
     anyw = pl.BlockSpec(memory_space=pl.ANY)
@@ -370,7 +374,7 @@
             jax.ShapeDtypeStruct((8, 128), i32),
             jax.ShapeDtypeStruct((1, 128), f32),
         ),
-        in_specs=[smem] * 3 + [vmem] * 2 + [anyw] * 2,
+        in_specs=[smem] * 3 + [vmem] * 9 + [anyw] * 2,
         out_specs=(anyw, vmem, vmem, vmem, vmem),
         scratch_shapes=[
             pltpu.VMEM((NJ, ROWS, 256), f32),
@@ -382,6 +386,7 @@
             pltpu.VMEM((NP, 256, 128), f32),
             pltpu.VMEM((NP, 256, 256), bf16),
             pltpu.VMEM((NP, 128, 128), f32),
+            pltpu.VMEM((8, 128), f32),
             pltpu.VMEM((NI, 1, 128), i32),
             pltpu.VMEM((NJ, 1, 128), i32),
             dma((5,)),
@@ -393,22 +398,24 @@
             dma((4,)),
         ],
         compiler_params=pltpu.CompilerParams(collective_id=0, has_side_effects=True, vmem_limit_bytes=VMEM_ALL),
-    )(occ, cnt, eo, tab, en, factors, vecs)
+    )(occ, cnt, eo, *lists, en, factors, vecs)
 
 
 UNROLL = 8
 SLOTS = NI * CAPI + NJ * CAPJ
 
 
-def couple(plan, weight, corr, arrived, term):
+def couple(plan, weight, corr, arrived, term, ready=None):
     term[NC] = jnp.zeros((128, 128), f32)
 
     def body(b, run):
         places = [b * UNROLL + k for k in range(UNROLL)]
+        if ready is not None:
+            ready(places)
         corrs = [split(corr[plan[0, s]]) for s in places]
         stage = []
         for s, (mh, ml) in zip(places, corrs):
-            xh, xl = split(arrived[plan[1, s]])
+            xh, xl = split(arrived[plan[1, s] if ready is None else s])
             xx = jnp.concatenate([xh, xl], axis=1)
             stage.append((jnp.concatenate([mh, ml], axis=1), jnp.concatenate([xx, xx], axis=0)))
         stage = [dot(m, x) for m, x in stage]
@@ -428,8 +435,8 @@
 
 
 def iterate_kernel(
-    qi, qj, plan, weight, occ, cnt, eo, en, amp0, ci, cj, amp_out, res_out,
-    amp, inv, corr, delta, term, snd_i, snd_j, mid, rcv0, rcv1, ls, si, ri, sj, rj,
+    qi, qj, plan, weight, occ, cnt, eo, en, amp0, ci, cj, amp_out, inv_out, held,
+    amp, inv, corr, delta, term, snd_i, snd_j, mid, rcv0, mine, ls, hs, si, ri, sj, rj,
 ):
     u = lax.axis_index("occi")
     v = lax.axis_index("occj")
@@ -450,7 +457,7 @@
 
     def exchange(it, src, arrived, beside):
         half_rows = CAPJ // 2
-        first, rest, sent = {}, [], []
+        first, rest, sent, kept = {}, [], [], []
 
         def fill(half, d):
             for e in range(4):
@@ -510,10 +517,17 @@
         for half in (0, 1):
             fill(half, 0)
             onward(half, 0)
+        stay = []
         for s in range(CAPI):
-            arrived[u * CAPI + s] = src[qi[u, 0, s]]
+            mine[s] = src[qi[u, 0, s]]
         for s in range(CAPJ):
-            arrived[NI * CAPI + v * CAPJ + s] = src[qj[v, 0, s]]
+            mine[CAPI + s] = src[qj[v, 0, s]]
+        stay.append((mine.at[pl.ds(0, CAPI)], u * CAPI, CAPI))
+        stay.append((mine.at[pl.ds(CAPI, CAPJ)], NI * CAPI + v * CAPJ, CAPJ))
+        for n, (a, at, size) in enumerate(stay):
+            c = pltpu.make_async_copy(a, arrived.at[pl.ds(at, size)], hs.at[it, n])
+            c.start()
+            kept.append(c)
         beside(0)
         for d in (1, 3, 2):
             for half in (0, 1):
@@ -524,13 +538,20 @@
         for half in (0, 1):
             for d in (1, 3, 2):
                 frm = vid(0, (4 - d) % 4) if half == 0 else vid((4 - d) % 4, 0)
-                for s in range(half_rows):
-                    arrived[NI * CAPI + frm * CAPJ + half_rows * half + s] = mid[it, half, d, s]
+                c = pltpu.make_async_copy(
+                    mid.at[it, half, d, pl.ds(0, half_rows)],
+                    arrived.at[pl.ds(NI * CAPI + frm * CAPJ + half_rows * half, half_rows)],
+                    hs.at[it, 2 + 4 * half + d],
+                )
+                c.start()
+                kept.append(c)
         beside(2)
         for c in rest:
             c.wait_recv()
         for c in sent:
             c.wait_send()
+        for c in kept:
+            c.wait()
 
     def inverses(lo, hi):
         def body(p, carry):
@@ -563,17 +584,59 @@
 
     lax.fori_loop(0, NP // 4, first, 0)
 
+    outs = [pltpu.make_async_copy(amp, amp_out, ls.at[3]), pltpu.make_async_copy(inv, inv_out, ls.at[4])]
+
     def beside1(part):
-        if part == 1:
-
-            def add(p, carry):
-                amp[p] = amp[p] + delta[p]
+        if part == 0:
+            outs[1].start()
+        elif part == 1:
+
+            def add(b, carry):
+                for k in range(4):
+                    p = 4 * b + k
+                    amp[p] = amp[p] + delta[p]
                 return carry
 
-            lax.fori_loop(0, NP, add, 0)
-
-    exchange(1, delta, rcv1, beside1)
-    couple(plan, weight, corr, rcv1, term)
+            lax.fori_loop(0, NP // 4, add, 0)
+            outs[0].start()
+
+    exchange(1, delta, held, beside1)
+    for c in outs:
+        c.wait()
+
+
+def finish_kernel(plan, weight, cnt, amp0, inv0, held, ci, cj, amp_out, res_out, amp, inv, corr, arrived, term, ls, cs, gs, os):
+    loads = [pltpu.make_async_copy(amp0, amp, ls.at[0]), pltpu.make_async_copy(inv0, inv, ls.at[1])]
+    mats = [
+        pltpu.make_async_copy(ci, corr.at[pl.ds(0, 32)], cs.at[0]),
+        pltpu.make_async_copy(cj, corr.at[pl.ds(32, 32)], cs.at[1]),
+    ]
+
+    def fetch(s):
+        return pltpu.make_async_copy(held.at[plan[1, s]], arrived.at[s], gs.at[s])
+
+    def start(b, carry):
+        for k in range(UNROLL):
+            fetch(b * UNROLL + k).start()
+        return carry
+
+    def ready(places):
+        for s in places:
+            fetch(s).wait()
+
+    lax.fori_loop(0, 1, start, 0)
+    for c in mats:
+        c.start()
+    lax.fori_loop(1, NC // UNROLL, start, 0)
+    for c in loads:
+        c.start()
+    for c in mats:
+        c.wait()
+    couple(plan, weight, corr, arrived, term, ready)
+    for c in loads:
+        c.wait()
+    rows = lax.broadcasted_iota(jnp.int32, (128, 128), 0)
+    cols = lax.broadcasted_iota(jnp.int32, (128, 128), 1)
 
     def second(b, carry):
         for k in range(4):
@@ -584,12 +647,31 @@
             inv[p] = jnp.where((rows < n) & (cols < n), -s, 0.0)
         return carry
 
-    lax.fori_loop(0, NP // 4, second, 0)
-    outs = [pltpu.make_async_copy(amp, amp_out, ls.at[0]), pltpu.make_async_copy(inv, res_out, ls.at[1])]
-    for c in outs:
-        c.start()
+    outs = []
+    for k in range(4):
+        lax.fori_loop(4 * k, 4 * k + 4, second, 0)
+        part = pl.ds(16 * k, 16)
+        outs.append(pltpu.make_async_copy(amp.at[part], amp_out.at[part], os.at[0, k]))
+        outs.append(pltpu.make_async_copy(inv.at[part], res_out.at[part], os.at[1, k]))
+        outs[-2].start()
+        outs[-1].start()
     for c in outs:
         c.wait()
+
+
+def finish(plan, weight, cnt, amp, inv, held, ci, cj):
+    smem = pl.BlockSpec(memory_space=pltpu.SMEM)
+    anyw = pl.BlockSpec(memory_space=pl.ANY)
+    dma = pltpu.SemaphoreType.DMA
+    mats = lambda *n: pltpu.VMEM(n + (128, 128), f32)
+    return pl.pallas_call(
+        finish_kernel,
+        out_shape=(jax.ShapeDtypeStruct((NP, 128, 128), f32),) * 2,
+        in_specs=[smem] * 3 + [anyw] * 5,
+        out_specs=(anyw, anyw),
+        scratch_shapes=[mats(NP), mats(NP), mats(NC), mats(NC), mats(NC + 1), dma((2,)), dma((2,)), dma((NC,)), dma((2, 4))],
+        compiler_params=pltpu.CompilerParams(vmem_limit_bytes=VMEM_ALL),
+    )(plan, weight, cnt, amp, inv, held, ci, cj)
 
 
 def iterate(qi, qj, plan, weight, occ, cnt, eo, en, amp, ci, cj):
@@ -600,9 +682,9 @@
     mats = lambda *n: pltpu.VMEM(n + (128, 128), f32)
     return pl.pallas_call(
         iterate_kernel,
-        out_shape=(jax.ShapeDtypeStruct((NP, 128, 128), f32),) * 2,
+        out_shape=(jax.ShapeDtypeStruct((NP, 128, 128), f32),) * 2 + (jax.ShapeDtypeStruct((SLOTS, 128, 128), f32),),
         in_specs=[smem] * 7 + [vmem] + [anyw] * 3,
-        out_specs=(anyw, anyw),
+        out_specs=(anyw,) * 3,
         scratch_shapes=[
             mats(NP),
             mats(NP),
@@ -613,8 +695,9 @@
             mats(2, 2, 4, 2 * CAPJ),
             mats(2, 2, 4, 2 * CAPJ),
             mats(SLOTS),
-            mats(SLOTS),
-            dma((3,)),
+            mats(CAPI + CAPJ),
+            dma((5,)),
+            dma((2, 10)),
             dma((2, 7)),
             dma((2, 7)),
             dma((2, 2, 4, 4)),
@@ -624,31 +707,23 @@
     )(qi, qj, plan, weight, occ, cnt, eo, en, amp, ci, cj)
 
 
-def row(i_list, j_list, fill):
-    rest = jnp.full((128 - 64,), fill, f32)
-    return jnp.concatenate([i_list.astype(f32), j_list.astype(f32), rest])
-
-
 def local(
     factors, pno_vecs, pair_occ, pno_count, pno_energy, occ_energy,
     coupi_peer, coupi_slot, coupi_target, coupi_fock, coupi_correlation,
     coupj_peer, coupj_slot, coupj_target, coupj_fock, coupj_correlation,
 ):
-    none = jnp.zeros((128,), f32)
-    tab = jnp.stack(
-        [
-            row(coupi_peer[:, 0], coupj_peer[:, 0] + NI, -1.0),
-            row(coupi_slot, coupj_slot, 0.0),
-            row(coupi_target, coupj_target, 1000.0),
-            row(coupi_fock, coupj_fock, 0.0),
-            none, none, none, none,
-        ]
-    )
+    lists = [
+        a.reshape(1, 32)
+        for a in (
+            coupi_peer, coupj_peer, coupi_slot, coupj_slot, coupi_target, coupj_target, coupi_fock, coupj_fock,
+        )
+    ]
     occ = pair_occ.T
-    amp, qi, qj, plan, weight = integrals(occ, pno_count, occ_energy, tab, pno_energy, factors, pno_vecs)
-    return iterate(
+    amp, qi, qj, plan, weight = integrals(occ, pno_count, occ_energy, lists, pno_energy, factors, pno_vecs)
+    amp, inv, held = iterate(
         qi, qj, plan, weight, occ, pno_count, occ_energy, pno_energy, amp, coupi_correlation, coupj_correlation
     )
+    return finish(plan, weight, pno_count, amp, inv, held, coupi_correlation, coupj_correlation)
 
 
 def solution(mesh):

time: 206 us -> 197 us (0.956)
  local copies, waits for them, and re-layouts: 7.48 us -> 0 us
  other arithmetic: 4.13 us -> 0 us
    pallas_call x0 -> x1, Pallas kernels: none -> 12.8 us  [finish(): pl.pallas_call(finish_kernel, out_shape=(jax.ShapeDtypeStruct((NP, 128, 1...]
    pallas_call x1, Pallas kernels: 119 us -> 109 us  [iterate(): pl.pallas_call(iterate_kernel, out_shape=(jax.ShapeDtypeStruct((NP, 128,...]
    unnamed x4 -> x0, local copies, waits for them, and re-layouts: 6.87 us -> none
    convert_element_type x5 -> x0, other arithmetic: 3.31 us -> none  [row(): return jnp.concatenate([i_list.astype(f32), j_list.astype(f32), rest])]
where the time goes in v4:
time: 197 us; the launch traced here: 196 us
  Pallas kernels  195 us (99%)
    pallas_call x1, Pallas kernels, iterate(): pl.pallas_call(iterate_kernel, out_shape=(jax.ShapeDtypeStruct((NP, 128,...  109 us
    pallas_call x1, Pallas kernels, integrals(): pl.pallas_call(integral_kernel, out_shape=(jax.ShapeDtypeStruct((NP, 128,...  73.8 us
    pallas_call x1, Pallas kernels, finish(): pl.pallas_call(finish_kernel, out_shape=(jax.ShapeDtypeStruct((NP, 128, 1...  12.8 us

profile of v4, /device:TPU:1, one launch (start us, length us, event | category | flops | bytes accessed | tf_op | source)
XLA Modules:
  0.0 196.2 jit_solution(8786666911701147010)
XLA Ops:
  0.6 73.8 %shard_map.167 = (f32[64,128,128]{2,1,0:T(8,128)}, s32[8,1,128]{2,1,0:T(1,128)}, s32[16,1,128]{2,1,0:T(1,128)}, s32[8,128]{1,0:T(8,128)}, f32[1,128]{1,0:T(1,128)}) custom-call(s32[2,64]{1,0:T(2,128)} %bitcast.9, s32[64]{0:T(128)} %cnt.5, f32[128]{0:T(128)} %eo.3, s32[1,32]{1,0:T(1,128)} %bitcast.11, s32[1,32]{1,0:T(1,128)} %bitcast.12, s32[1,32]{1,0:T(1,128)} %bitcast.13, ...), custom_call_target="tpu_custom_call" | custom-call | tf_op jit(solution)/shard_map/pallas_call | solution.py:368
  74.5 108.8 %shard_map.168 = (f32[64,128,128]{2,1,0:T(8,128)}, f32[64,128,128]{2,1,0:T(8,128)}, f32[128,128,128]{2,1,0:T(8,128)}) custom-call(s32[8,1,128]{2,1,0:T(1,128)} %get-tuple-element.12.qi, s32[16,1,128]{2,1,0:T(1,128)} %get-tuple-element.13.qj, s32[8,128]{1,0:T(8,128)} %get-tuple-element.10.plan, f32[1,128]{1,0:T(1,128)} %get-tuple-element.11.weight, ...), custom_call_target="tpu_custom_call" | custom-call | tf_op jit(solution)/shard_map/pallas_call | solution.py:683
  183.2 12.8 %shard_map.169 = (f32[64,128,128]{2,1,0:T(8,128)}, f32[64,128,128]{2,1,0:T(8,128)}) custom-call(s32[8,128]{1,0:T(8,128)} %get-tuple-element.10.plan, f32[1,128]{1,0:T(1,128)} %get-tuple-element.11.weight, s32[64]{0:T(128)} %cnt.5, f32[64,128,128]{2,1,0:T(8,128)} %get-tuple-element.15.amp0, f32[64,128,128]{2,1,0:T(8,128)} %get-tuple-element.16.inv0, ...), custom_call_target="tpu_custom_call" | custom-call | tf_op jit(solution)/shard_map/pallas_call | solution.py:667

commit v5 on v4

--- a/solution.py
+++ b/solution.py
@@ -14,8 +14,9 @@
 CAPI, CAPJ = 8, 4
 NP = 64
 NC = 64
-WAVES = 2
-ROWS = 512 // WAVES
+SIZES = (192, 192, 128)
+STARTS = (0, 192, 384)
+WAVES = len(SIZES)
 VMEM_ALL = 60 * 2**20
 GROUP = 8
 
@@ -99,15 +100,13 @@
 
 
 def integral_kernel(
-    occ, cnt, eo, pi, pj, si, sj, ti, tj, ki, kj, en, fac, vecs, amp, qi, qj, plan, weight,
-    fi0, fi1, fj0, fj1, th0, th1, tl0, tl1, jh0, jh1, jl0, jl1, vec, both, acc, tab, ri, rj, own_sem, tab_sem, rs, ss, crs, css, out_sem,
+    occ, cnt, eo, pi, pj, si, sj, ti, tj, ki, kj, en, fac, vecs, amp, inv_out, qi, qj, plan, weight,
+    fi, fj, th, tl, jh, jl, vec, both, acc, inv, tab, ri, rj, own_sem, tab_sem, rs, ss, crs, css, out_sem,
 ):
     u = lax.axis_index("occi")
     v = lax.axis_index("occj")
     x, z = v % 4, v // 4
     y, core = u // 2, u % 2
-    fi, fj = (fi0, fi1), (fj0, fj1)
-    th, tl, jh, jl = (th0, th1), (tl0, tl1), (jh0, jh1), (jl0, jl1)
 
     def vid(zz, xx):
         return ((z + zz) % 4) * 4 + (x + xx) % 4
@@ -117,7 +116,7 @@
 
     own = [pltpu.make_async_copy(vecs, vec, own_sem.at[0])]
     for w in range(WAVES):
-        at = fac.at[0, pl.ds(w * ROWS, ROWS)]
+        at = fac.at[0, pl.ds(STARTS[w], SIZES[w])]
         own.append(pltpu.make_async_copy(at, fi[w].at[v], own_sem.at[1 + 2 * w]))
         own.append(pltpu.make_async_copy(at, fj[w].at[u], own_sem.at[2 + 2 * w]))
     greet(u, v)
@@ -127,7 +126,7 @@
 
     def send(w, from_fac, buf, slot, q, n, sem, dev):
         at = buf[w].at[slot, pl.ds(q, n)]
-        src = fac.at[0, pl.ds(w * ROWS + q, n)] if from_fac else at
+        src = fac.at[0, pl.ds(STARTS[w] + q, n)] if from_fac else at
         c = pltpu.make_async_remote_copy(src, at, sem[0], sem[1], dev, MESH)
         c.start()
         pending.append(c)
@@ -137,7 +136,8 @@
         pltpu.make_async_remote_copy(at, at, sem[0], sem[1], dev, MESH).wait_recv()
 
     def wave(w):
-        h = ROWS // 2
+        size = SIZES[w]
+        h = size // 2
         s = h // 2
 
         def sem(half, k):
@@ -174,9 +174,9 @@
                 send(w, True, fi, v, q, h, sem(half, 1), first(3))
             for half, q, first, second, slot in halves:
                 second_send(half, q, second, slot, 0, 4, True)
-            send(w, True, fj, u, 0, ROWS, csem(0), {"occi": uid(1, 0)})
-            send(w, True, fj, u, 0, ROWS, csem(1), {"occi": uid(3, 0)})
-            send(w, True, fj, u, 0, ROWS, csem(4), {"occi": uid(0, 1)})
+            send(w, True, fj, u, 0, size, csem(0), {"occi": uid(1, 0)})
+            send(w, True, fj, u, 0, size, csem(1), {"occi": uid(3, 0)})
+            send(w, True, fj, u, 0, size, csem(4), {"occi": uid(0, 1)})
 
         def s1():
             for half, q, first, second, slot in halves:
@@ -191,13 +191,13 @@
         def s2():
             for half, q, first, second, slot in halves:
                 second_forward(half, q, second, slot, 0, 4)
-            n = ROWS // 2
-            got(w, fj, uid(3, 0), 0, ROWS, csem(0), {"occi": uid(1, 0)})
+            n = size // 2
+            got(w, fj, uid(3, 0), 0, size, csem(0), {"occi": uid(1, 0)})
             send(w, False, fj, uid(3, 0), 0, n, csem(2), {"occi": uid(1, 0)})
-            send(w, False, fj, uid(3, 0), 0, ROWS, csem(5), {"occi": uid(0, 1)})
-            got(w, fj, uid(1, 0), 0, ROWS, csem(1), {"occi": uid(1, 0)})
+            send(w, False, fj, uid(3, 0), 0, size, csem(5), {"occi": uid(0, 1)})
+            got(w, fj, uid(1, 0), 0, size, csem(1), {"occi": uid(1, 0)})
             send(w, False, fj, uid(1, 0), n, n, csem(3), {"occi": uid(3, 0)})
-            send(w, False, fj, uid(1, 0), 0, ROWS, csem(6), {"occi": uid(0, 1)})
+            send(w, False, fj, uid(1, 0), 0, size, csem(6), {"occi": uid(0, 1)})
 
         def s3():
             for half, q, first, second, slot in halves:
@@ -209,10 +209,10 @@
             for half, q, first, second, slot in halves:
                 second_forward(half, q, second, slot, 3, 8)
                 second_forward(half, q, second, slot, 1, 12)
-            n = ROWS // 2
+            n = size // 2
             got(w, fj, uid(2, 0), 0, n, csem(2), {"occi": uid(1, 0)})
             got(w, fj, uid(2, 0), n, n, csem(3), {"occi": uid(1, 0)})
-            send(w, False, fj, uid(2, 0), 0, ROWS, csem(7), {"occi": uid(0, 1)})
+            send(w, False, fj, uid(2, 0), 0, size, csem(7), {"occi": uid(0, 1)})
 
         def s5():
             for half, q, first, second, slot in halves:
@@ -224,7 +224,7 @@
                     got(w, fi, slot(a, 2), q, s, sem(half, base + 2), second(1))
                     got(w, fi, slot(a, 2), q + s, s, sem(half, base + 3), second(1))
             for k, yy in ((4, 0), (5, 3), (6, 1), (7, 2)):
-                got(w, fj, uid(yy, 1), 0, ROWS, csem(k), {"occi": uid(0, 1)})
+                got(w, fj, uid(yy, 1), 0, size, csem(k), {"occi": uid(0, 1)})
 
         return s0, s1, s2, s3, s4, s5, s6
 
@@ -251,6 +251,18 @@
 
     rows = lax.broadcasted_iota(jnp.int32, (128, 128), 0)
     cols = lax.broadcasted_iota(jnp.int32, (128, 128), 1)
+
+    def inverses():
+        def body(b, c):
+            group = [4 * b + k for k in range(4)]
+            sums = [denominator(en, p) for p in group]
+            for p, den in zip(group, sums):
+                n = cnt[p]
+                den = den - (eo[occ[0, p]] + eo[occ[1, p]])
+                inv[p] = jnp.where((rows < n) & (cols < n), 1.0 / den, 0.0)
+            return c
+
+        lax.fori_loop(0, NP // 4, body, 0)
 
     def some(w, lo, hi):
         def body(b, c):
@@ -274,11 +286,12 @@
                 for p, o in zip(group, stage):
                     acc[p] = o
                 return c
-            sums = [denominator(en, p) for p in group]
-            for p, o, den in zip(group, stage, sums):
-                den = den - (eo[occ[0, p]] + eo[occ[1, p]])
-                n = cnt[p]
-                acc[p] = jnp.where((rows < n) & (cols < n), -(acc[p] + o) / den, 0.0)
+            if w < WAVES - 1:
+                for p, o in zip(group, stage):
+                    acc[p] = acc[p] + o
+                return c
+            for p, o in zip(group, stage):
+                acc[p] = -(acc[p] + o) * inv[p]
             return c
 
         lax.fori_loop(lo // GROUP, hi // GROUP, body, 0)
@@ -286,7 +299,7 @@
     near = [(0, 0), (0, 1), (0, 3), (1, 0), (3, 0)]
     middle = [(1, 1), (1, 3), (3, 1), (3, 3)]
     far = [(0, 2), (2, 0), (1, 2), (3, 2), (2, 1), (2, 3), (2, 2)]
-    a, b = wave(0), wave(1)
+    a, b, c3 = wave(0), wave(1), wave(2)
     a[0]()
     for r, (one, two, fill) in enumerate(((pi, pj, -1.0), (si, sj, 0.0), (ti, tj, 1000.0), (ki, kj, 0.0))):
         tab[pl.ds(r, 1), :] = jnp.full((1, 128), fill, f32)
@@ -318,11 +331,15 @@
         c.wait()
     halve_i(0, near)
     a[4]()
+    inverses()
+    keep = pltpu.make_async_copy(inv, inv_out, out_sem.at[4])
+    keep.start()
     halve_i(0, middle)
     a[5]()
     b[2]()
     halve_i(1, near)
     b[3]()
+    c3[0]()
     a[6]()
     halve_i(0, far)
     halve_j(0)
@@ -330,14 +347,27 @@
     b[4]()
     some(0, 16, 32)
     b[5]()
+    c3[1]()
     some(0, 32, 64)
     halve_i(1, middle)
+    c3[2]()
+    halve_i(2, near)
+    c3[3]()
     b[6]()
     halve_i(1, far)
     halve_j(1)
-    outs = []
+    some(1, 0, 16)
+    c3[4]()
+    some(1, 16, 32)
+    c3[5]()
+    some(1, 32, 64)
+    halve_i(2, middle)
+    c3[6]()
+    halve_i(2, far)
+    halve_j(2)
+    outs = [keep]
     for k in range(4):
-        some(1, 16 * k, 16 * k + 16)
+        some(WAVES - 1, 16 * k, 16 * k + 16)
         part = pl.ds(16 * k, 16)
         c = pltpu.make_async_copy(acc.at[part], amp.at[part], out_sem.at[k])
         c.start()
@@ -369,33 +399,35 @@
         integral_kernel,
         out_shape=(
             jax.ShapeDtypeStruct((NP, 128, 128), f32),
+            jax.ShapeDtypeStruct((NP, 128, 128), f32),
             jax.ShapeDtypeStruct((NI, 1, 128), i32),
             jax.ShapeDtypeStruct((NJ, 1, 128), i32),
             jax.ShapeDtypeStruct((8, 128), i32),
             jax.ShapeDtypeStruct((1, 128), f32),
         ),
         in_specs=[smem] * 3 + [vmem] * 9 + [anyw] * 2,
-        out_specs=(anyw, vmem, vmem, vmem, vmem),
+        out_specs=(anyw, anyw, vmem, vmem, vmem, vmem),
         scratch_shapes=[
-            pltpu.VMEM((NJ, ROWS, 256), f32),
-            pltpu.VMEM((NJ, ROWS, 256), f32),
-            pltpu.VMEM((NI, ROWS, 256), f32),
-            pltpu.VMEM((NI, ROWS, 256), f32),
-            *[pltpu.VMEM((NJ, ROWS, 256), bf16)] * 4,
-            *[pltpu.VMEM((NI, ROWS, 256), bf16)] * 4,
+            [pltpu.VMEM((NJ, n, 256), f32) for n in SIZES],
+            [pltpu.VMEM((NI, n, 256), f32) for n in SIZES],
+            [pltpu.VMEM((NJ, n, 256), bf16) for n in SIZES],
+            [pltpu.VMEM((NJ, n, 256), bf16) for n in SIZES],
+            [pltpu.VMEM((NI, n, 256), bf16) for n in SIZES],
+            [pltpu.VMEM((NI, n, 256), bf16) for n in SIZES],
             pltpu.VMEM((NP, 256, 128), f32),
             pltpu.VMEM((NP, 256, 256), bf16),
+            pltpu.VMEM((NP, 128, 128), f32),
             pltpu.VMEM((NP, 128, 128), f32),
             pltpu.VMEM((8, 128), f32),
             pltpu.VMEM((NI, 1, 128), i32),
             pltpu.VMEM((NJ, 1, 128), i32),
-            dma((5,)),
+            dma((1 + 2 * WAVES,)),
             dma((2, 22)),
             dma((WAVES, 2, 20)),
             dma((WAVES, 2, 20)),
             dma((WAVES, 8)),
             dma((WAVES, 8)),
-            dma((4,)),
+            dma((5,)),
         ],
         compiler_params=pltpu.CompilerParams(collective_id=0, has_side_effects=True, vmem_limit_bytes=VMEM_ALL),
     )(occ, cnt, eo, *lists, en, factors, vecs)
@@ -435,18 +467,17 @@
 
 
 def iterate_kernel(
-    qi, qj, plan, weight, occ, cnt, eo, en, amp0, ci, cj, amp_out, inv_out, held,
+    qi, qj, plan, weight, amp0, inv0, ci, cj, amp_out, held,
     amp, inv, corr, delta, term, snd_i, snd_j, mid, rcv0, mine, ls, hs, si, ri, sj, rj,
 ):
     u = lax.axis_index("occi")
     v = lax.axis_index("occj")
     x, z = v % 4, v // 4
-    rows = lax.broadcasted_iota(jnp.int32, (128, 128), 0)
-    cols = lax.broadcasted_iota(jnp.int32, (128, 128), 1)
     loads = [
         pltpu.make_async_copy(amp0, amp, ls.at[0]),
         pltpu.make_async_copy(ci, corr.at[pl.ds(0, 32)], ls.at[1]),
         pltpu.make_async_copy(cj, corr.at[pl.ds(32, 32)], ls.at[2]),
+        pltpu.make_async_copy(inv0, inv, ls.at[4]),
     ]
     for c in loads:
         c.start()
@@ -553,22 +584,8 @@
         for c in kept:
             c.wait()
 
-    def inverses(lo, hi):
-        def body(p, carry):
-            den = denominator(en, p) - (eo[occ[0, p]] + eo[occ[1, p]])
-            n = cnt[p]
-            inv[p] = jnp.where((rows < n) & (cols < n), 1.0 / den, 0.0)
-            return carry
-
-        lax.fori_loop(lo, hi, body, 0)
-
     def beside0(part):
-        if part == 0:
-            inverses(0, 16)
-        elif part == 1:
-            inverses(16, 32)
-        else:
-            inverses(32, 64)
+        if part == 2:
             for c in loads[1:]:
                 c.wait()
 
@@ -584,12 +601,10 @@
 
     lax.fori_loop(0, NP // 4, first, 0)
 
-    outs = [pltpu.make_async_copy(amp, amp_out, ls.at[3]), pltpu.make_async_copy(inv, inv_out, ls.at[4])]
+    out = pltpu.make_async_copy(amp, amp_out, ls.at[3])
 
     def beside1(part):
-        if part == 0:
-            outs[1].start()
-        elif part == 1:
+        if part == 1:
 
             def add(b, carry):
                 for k in range(4):
@@ -598,11 +613,10 @@
                 return carry
 
             lax.fori_loop(0, NP // 4, add, 0)
-            outs[0].start()
+            out.start()
 
     exchange(1, delta, held, beside1)
-    for c in outs:
-        c.wait()
+    out.wait()
 
 
 def finish_kernel(plan, weight, cnt, amp0, inv0, held, ci, cj, amp_out, res_out, amp, inv, corr, arrived, term, ls, cs, gs, os):
@@ -674,7 +688,7 @@
     )(plan, weight, cnt, amp, inv, held, ci, cj)
 
 
-def iterate(qi, qj, plan, weight, occ, cnt, eo, en, amp, ci, cj):
+def iterate(qi, qj, plan, weight, amp, inv, ci, cj):
     smem = pl.BlockSpec(memory_space=pltpu.SMEM)
     vmem = pl.BlockSpec(memory_space=pltpu.VMEM)
     anyw = pl.BlockSpec(memory_space=pl.ANY)
@@ -682,9 +696,9 @@
     mats = lambda *n: pltpu.VMEM(n + (128, 128), f32)
     return pl.pallas_call(
         iterate_kernel,
-        out_shape=(jax.ShapeDtypeStruct((NP, 128, 128), f32),) * 2 + (jax.ShapeDtypeStruct((SLOTS, 128, 128), f32),),
-        in_specs=[smem] * 7 + [vmem] + [anyw] * 3,
-        out_specs=(anyw,) * 3,
+        out_shape=(jax.ShapeDtypeStruct((NP, 128, 128), f32), jax.ShapeDtypeStruct((SLOTS, 128, 128), f32)),
+        in_specs=[smem] * 4 + [anyw] * 4,
+        out_specs=(anyw,) * 2,
         scratch_shapes=[
             mats(NP),
             mats(NP),
@@ -704,7 +718,7 @@
             dma((2, 2, 4, 4)),
         ],
         compiler_params=pltpu.CompilerParams(collective_id=1, has_side_effects=True, vmem_limit_bytes=VMEM_ALL),
-    )(qi, qj, plan, weight, occ, cnt, eo, en, amp, ci, cj)
+    )(qi, qj, plan, weight, amp, inv, ci, cj)
 
 
 def local(
@@ -719,10 +733,8 @@
         )
     ]
     occ = pair_occ.T
-    amp, qi, qj, plan, weight = integrals(occ, pno_count, occ_energy, lists, pno_energy, factors, pno_vecs)
-    amp, inv, held = iterate(
-        qi, qj, plan, weight, occ, pno_count, occ_energy, pno_energy, amp, coupi_correlation, coupj_correlation
-    )
+    amp, inv, qi, qj, plan, weight = integrals(occ, pno_count, occ_energy, lists, pno_energy, factors, pno_vecs)
+    amp, held = iterate(qi, qj, plan, weight, amp, inv, coupi_correlation, coupj_correlation)
     return finish(plan, weight, pno_count, amp, inv, held, coupi_correlation, coupj_correlation)
 
 

time: 197 us -> 193 us (0.980)
  Pallas kernels: 195 us -> 192 us
    pallas_call x1, Pallas kernels: 73.8 us -> 70.5 us  [integrals(): pl.pallas_call(integral_kernel, out_shape=(jax.ShapeDtypeStruct((NP, 128,...]
where the time goes in v5:
time: 193 us
  Pallas kernels  192 us (99%)
    pallas_call x1, Pallas kernels, iterate(): pl.pallas_call(iterate_kernel, out_shape=(jax.ShapeDtypeStruct((NP, 128,...  109 us
    pallas_call x1, Pallas kernels, integrals(): pl.pallas_call(integral_kernel, out_shape=(jax.ShapeDtypeStruct((NP, 128,...  70.5 us
    pallas_call x1, Pallas kernels, finish(): pl.pallas_call(finish_kernel, out_shape=(jax.ShapeDtypeStruct((NP, 128, 1...  12.8 us

profile of v5, /device:TPU:1, one launch (start us, length us, event | category | flops | bytes accessed | tf_op | source)
XLA Modules:
  0.0 193.1 jit_solution(13651150642179482758)
XLA Ops:
  0.6 70.5 %shard_map.167 = (f32[64,128,128]{2,1,0:T(8,128)}, f32[64,128,128]{2,1,0:T(8,128)}, s32[8,1,128]{2,1,0:T(1,128)}, s32[16,1,128]{2,1,0:T(1,128)}, s32[8,128]{1,0:T(8,128)}, /*index=5*/f32[1,128]{1,0:T(1,128)}) custom-call(s32[2,64]{1,0:T(2,128)} %bitcast.9, s32[64]{0:T(128)} %cnt.3, f32[128]{0:T(128)} %eo.1, s32[1,32]{1,0:T(1,128)} %bitcast.10, ...), custom_call_target="tpu_custom_call" | custom-call | tf_op jit(solution)/shard_map/pallas_call | solution.py:398
  71.1 109.0 %shard_map.168 = (f32[64,128,128]{2,1,0:T(8,128)}, f32[128,128,128]{2,1,0:T(8,128)}) custom-call(s32[8,1,128]{2,1,0:T(1,128)} %get-tuple-element.12.qi, s32[16,1,128]{2,1,0:T(1,128)} %get-tuple-element.13.qj, s32[8,128]{1,0:T(8,128)} %get-tuple-element.10.plan, f32[1,128]{1,0:T(1,128)} %get-tuple-element.11.weight, f32[64,128,128]{2,1,0:T(8,128)} %get-tuple-element.14.amp0, ...), custom_call_target="tpu_custom_call" | custom-call | tf_op jit(solution)/shard_map/pallas_call | solution.py:697
  180.1 12.8 %shard_map.169 = (f32[64,128,128]{2,1,0:T(8,128)}, f32[64,128,128]{2,1,0:T(8,128)}) custom-call(s32[8,128]{1,0:T(8,128)} %get-tuple-element.10.plan, f32[1,128]{1,0:T(1,128)} %get-tuple-element.11.weight, s32[64]{0:T(128)} %cnt.3, f32[64,128,128]{2,1,0:T(8,128)} %get-tuple-element.16.amp0, f32[64,128,128]{2,1,0:T(8,128)} %get-tuple-element.15.inv0, ...), custom_call_target="tpu_custom_call" | custom-call | tf_op jit(solution)/shard_map/pallas_call | solution.py:681

commit v6 on v5

--- a/solution.py
+++ b/solution.py
@@ -18,7 +18,7 @@
 STARTS = (0, 192, 384)
 WAVES = len(SIZES)
 VMEM_ALL = 60 * 2**20
-GROUP = 8
+GROUP = 16
 
 OFF_I = [(2, 0), (2, 1), (1, 0), (3, 0), (1, 1), (3, 1), (0, 1)]
 OFF_J = sorted(
@@ -433,7 +433,7 @@
     )(occ, cnt, eo, *lists, en, factors, vecs)
 
 
-UNROLL = 8
+UNROLL = 16
 SLOTS = NI * CAPI + NJ * CAPJ
 
 

time: 193 us -> 190 us (0.984)
  Pallas kernels: 192 us -> 189 us
    pallas_call x1, Pallas kernels: 70.5 us -> 68.3 us  [integrals(): pl.pallas_call(integral_kernel, out_shape=(jax.ShapeDtypeStruct((NP, 128,...]
where the time goes in v6:
time: 190 us
  Pallas kernels  189 us (99%)
    pallas_call x1, Pallas kernels, iterate(): pl.pallas_call(iterate_kernel, out_shape=(jax.ShapeDtypeStruct((NP, 128,...  108 us
    pallas_call x1, Pallas kernels, integrals(): pl.pallas_call(integral_kernel, out_shape=(jax.ShapeDtypeStruct((NP, 128,...  68.3 us
    pallas_call x1, Pallas kernels, finish(): pl.pallas_call(finish_kernel, out_shape=(jax.ShapeDtypeStruct((NP, 128, 1...  12.4 us

profile of v6, /device:TPU:1, one launch (start us, length us, event | category | flops | bytes accessed | tf_op | source)
XLA Modules:
  0.0 190.0 jit_solution(933888280713232601)
XLA Ops:
  0.6 68.3 %shard_map.167 = (f32[64,128,128]{2,1,0:T(8,128)}, f32[64,128,128]{2,1,0:T(8,128)}, s32[8,1,128]{2,1,0:T(1,128)}, s32[16,1,128]{2,1,0:T(1,128)}, s32[8,128]{1,0:T(8,128)}, /*index=5*/f32[1,128]{1,0:T(1,128)}) custom-call(s32[2,64]{1,0:T(2,128)} %bitcast.9, s32[64]{0:T(128)} %cnt.3, f32[128]{0:T(128)} %eo.1, s32[1,32]{1,0:T(1,128)} %bitcast.10, ...), custom_call_target="tpu_custom_call" | custom-call | tf_op jit(solution)/shard_map/pallas_call | solution.py:398
  69.0 108.4 %shard_map.168 = (f32[64,128,128]{2,1,0:T(8,128)}, f32[128,128,128]{2,1,0:T(8,128)}) custom-call(s32[8,1,128]{2,1,0:T(1,128)} %get-tuple-element.12.qi, s32[16,1,128]{2,1,0:T(1,128)} %get-tuple-element.13.qj, s32[8,128]{1,0:T(8,128)} %get-tuple-element.10.plan, f32[1,128]{1,0:T(1,128)} %get-tuple-element.11.weight, f32[64,128,128]{2,1,0:T(8,128)} %get-tuple-element.14.amp0, ...), custom_call_target="tpu_custom_call" | custom-call | tf_op jit(solution)/shard_map/pallas_call | solution.py:697
  177.4 12.4 %shard_map.169 = (f32[64,128,128]{2,1,0:T(8,128)}, f32[64,128,128]{2,1,0:T(8,128)}) custom-call(s32[8,128]{1,0:T(8,128)} %get-tuple-element.10.plan, f32[1,128]{1,0:T(1,128)} %get-tuple-element.11.weight, s32[64]{0:T(128)} %cnt.3, f32[64,128,128]{2,1,0:T(8,128)} %get-tuple-element.16.amp0, f32[64,128,128]{2,1,0:T(8,128)} %get-tuple-element.15.inv0, ...), custom_call_target="tpu_custom_call" | custom-call | tf_op jit(solution)/shard_map/pallas_call | solution.py:681
